TPU v7x, 128 devices: a whole 4x4x4 slice. The times are simulated.
128 devices in a mesh: sar: 8 (over y, core), opt: 16 (over z, x).
Axes of the slice: x: 4, y: 4, z: 4, core: 2. Of those that a mesh axis runs over, the one named last changes fastest.
Arguments:
- sar_tokens: bfloat16 [2048, 196, 512], P(('sar', 'opt')), may hold values from -600 to 600
- opt_tokens: bfloat16 [2048, 196, 512], P(('sar', 'opt')), may hold values from -600 to 600
- candidates: int32 [2048, 3], P(('sar', 'opt')), may hold values from 0 to 2047, as said below
Outputs:
- grad_sar: bfloat16 [2048, 196, 512], P(('sar', 'opt'))
- grad_opt: bfloat16 [2048, 196, 512], P(('sar', 'opt'))
Inputs may be any that keep to these rules, and one draw needn't show every extreme that they name: `candidates`: row i lists optical tiles of the same block of 256 tiles as SAR tile i (ids b * 256 to b * 256 + 255), never a tile of the aligned group of 16 tiles that holds i. Over one aligned group of 16 SAR tiles the lists name at most 2 distinct tiles of any other group, and exactly 2 of some group; ids may repeat.
All inputs are finite; a program needn't handle non-finite values.
Results may differ from a plain program's by a relative error of at most 0.0061.
Values may be sent and summed in bfloat16 or wider, within the bound.
A program may use at most 192 MiB of HBM per device.

v0:
```python
import jax
import jax.numpy as jnp
from jax import lax
from jax.sharding import PartitionSpec as P

NEG = 3
CAP = 2


EPSILON = 1e-06
POOL_TEMP = 0.02
CAND_TEMP = 0.1
NCE_TEMP = 0.07
LOSS_SCALE = 256.0
NCE_SCALE = 0.05 * 256.0 / 0.07


def unit_rows(tokens):
    values = tokens.astype(jnp.float32)
    inverse = lax.rsqrt(jnp.sum(values * values, axis=-1, keepdims=True) + EPSILON)
    return (values * inverse, inverse)


def pooled_unit(unit_tokens):
    mean_rows = jnp.mean(unit_tokens, axis=1)
    pool_scale = lax.rsqrt(jnp.sum(mean_rows * mean_rows, axis=-1, keepdims=True) + EPSILON)
    return (mean_rows * pool_scale, pool_scale)


def pair_grads(sar_rows, cand_rows):
    scores = jnp.einsum("ad,kbd->kab", sar_rows, cand_rows, preferred_element_type=jnp.float32)
    exponent = jnp.exp(scores / POOL_TEMP)
    totals = jnp.sum(exponent, axis=-1)
    match_score = POOL_TEMP * jnp.mean(jnp.log(totals), axis=-1)
    cand_weight = jnp.exp(match_score / CAND_TEMP)
    cand_prob = cand_weight / jnp.sum(cand_weight)
    target = (jnp.arange(cand_prob.shape[0]) == 0).astype(jnp.float32)
    pair_coef = LOSS_SCALE * (cand_prob - target) / CAND_TEMP
    length = sar_rows.shape[0]
    weights = ((pair_coef / length)[:, None, None] * exponent / totals[:, :, None]).astype(
        jnp.bfloat16
    )
    sar_part = jnp.einsum("kab,kbd->ad", weights, cand_rows, preferred_element_type=jnp.float32)
    cand_part = jnp.einsum("kab,ad->kbd", weights, sar_rows, preferred_element_type=jnp.float32)
    return (sar_part, cand_part)


def finish(unit_tokens, inverse, pool_rows, pool_scale, pair_grad, pool_grad):
    length = unit_tokens.shape[1]
    pooled_back = (
        pool_grad - pool_rows * jnp.sum(pool_rows * pool_grad, axis=-1, keepdims=True)
    ) * pool_scale
    total = pair_grad + pooled_back[:, None, :] / length
    back = (total - unit_tokens * jnp.sum(unit_tokens * total, axis=-1, keepdims=True)) * inverse
    return back.astype(jnp.bfloat16)


def per_device(sar_tokens, opt_tokens, candidates):
    tile_count, length, width = sar_tokens.shape
    groups = lax.axis_size("opt")
    block_size = tile_count * groups
    slot_total = groups * CAP
    sar_unit, sar_inverse = unit_rows(sar_tokens)
    opt_unit, opt_inverse = unit_rows(opt_tokens)
    sar_bf = sar_unit.astype(jnp.bfloat16)
    opt_bf = opt_unit.astype(jnp.bfloat16)
    local_ids = (candidates % block_size).reshape(-1)
    hit_table = (local_ids[:, None] == jnp.arange(block_size)[None, :]).astype(jnp.int32)
    needed = jnp.max(hit_table, axis=0).reshape(groups, tile_count)
    slot_rank = jnp.cumsum(needed, axis=1) - needed
    chosen = needed[:, :, None] * (slot_rank[:, :, None] == jnp.arange(CAP)[None, None, :]).astype(
        jnp.int32
    )
    asked_ids = jnp.sum(chosen * jnp.arange(tile_count)[None, :, None], axis=1)
    slot_table = (jnp.arange(groups)[:, None] * CAP + slot_rank).reshape(-1)
    request_slot = jnp.sum(hit_table * slot_table[None, :], axis=1).reshape(tile_count, NEG)
    asked = lax.all_to_all(asked_ids, "opt", split_axis=0, concat_axis=0, tiled=True)
    rows = opt_bf[asked]
    returned = lax.all_to_all(rows, "opt", split_axis=0, concat_axis=0, tiled=True)
    fetched = returned
    fetched = fetched.reshape(slot_total, length, width)
    per_turn = min(4, tile_count)
    turn_count = tile_count // per_turn

    def pair_step(slot_sums, inputs):
        sar_rows, own_rows, slot_rows = inputs
        cand_rows = jnp.concatenate([own_rows[:, None], fetched[slot_rows]], axis=1)
        sar_part, cand_part = jax.vmap(pair_grads)(sar_rows, cand_rows)
        slot_sums = slot_sums.at[slot_rows.reshape(-1)].add(
            cand_part[:, 1:].reshape(-1, length, width)
        )
        return (slot_sums, (sar_part, cand_part[:, 0]))

    start_sums = jnp.zeros((slot_total, length, width), jnp.float32)
    slot_sums, (sar_pair, own_pair) = lax.scan(
        pair_step,
        start_sums,
        (
            sar_bf.reshape(turn_count, per_turn, length, width),
            opt_bf.reshape(turn_count, per_turn, length, width),
            request_slot.reshape(turn_count, per_turn, NEG),
        ),
    )
    sar_pair = sar_pair.reshape(tile_count, length, width)
    own_pair = own_pair.reshape(tile_count, length, width)
    slot_round = slot_sums.astype(jnp.bfloat16).reshape(groups, CAP, length, width)
    returned_grads = lax.all_to_all(slot_round, "opt", split_axis=0, concat_axis=0, tiled=True)
    opt_pair = own_pair.at[asked.reshape(-1)].add(
        returned_grads.reshape(slot_total, length, width).astype(jnp.float32)
    )
    sar_pool, sar_scale = pooled_unit(sar_unit)
    opt_pool, opt_scale = pooled_unit(opt_unit)
    sar_pool_bf = sar_pool.astype(jnp.bfloat16)
    opt_pool_bf = opt_pool.astype(jnp.bfloat16)
    opt_all = lax.all_gather(opt_pool_bf, ("sar", "opt"), axis=0, tiled=True)
    row_ids = lax.axis_index(("sar", "opt")) * tile_count + jnp.arange(tile_count)
    col_ids = jnp.arange(opt_all.shape[0])
    logits = (
        lax.dot_general(
            sar_pool_bf, opt_all, (((1,), (1,)), ((), ())), preferred_element_type=jnp.float32
        )
        / NCE_TEMP
    )
    exp_logits = jnp.exp(logits)
    row_sums = jnp.sum(exp_logits, axis=1)
    diagonal = (row_ids[:, None] == col_ids[None, :]).astype(jnp.float32)
    nce_coef = (NCE_SCALE * (exp_logits / row_sums[:, None] - diagonal)).astype(jnp.bfloat16)
    sar_pool_grad = jnp.dot(nce_coef, opt_all, preferred_element_type=jnp.float32)
    opt_pool_grad = lax.psum_scatter(
        lax.dot_general(
            nce_coef, sar_pool_bf, (((0,), (0,)), ((), ())), preferred_element_type=jnp.float32
        ),
        ("sar", "opt"),
        scatter_dimension=0,
        tiled=True,
    )
    grad_sar = finish(sar_unit, sar_inverse, sar_pool, sar_scale, sar_pair, sar_pool_grad)
    grad_opt = finish(opt_unit, opt_inverse, opt_pool, opt_scale, opt_pair, opt_pool_grad)
    return (grad_sar, grad_opt)


def solution(mesh):
    placed = (P(("sar", "opt"), None, None), P(("sar", "opt"), None, None), P(("sar", "opt"), None))
    return jax.shard_map(
        per_device,
        mesh=mesh,
        in_specs=placed,
        out_specs=(P(("sar", "opt"), None, None), P(("sar", "opt"), None, None)),
        check_vma=False,
    )
```

profile of v0, /device:TPU:2, one launch (start us, length us, event | category | flops | bytes accessed | tf_op | source)
XLA Modules:
  0.0 925.1 jit_solution(8292930633300134677)
XLA Ops:
  9.2 8.3 all-to-all-start
  17.5 5.3 fusion.31
  23.5 3.3 fusion.22
  27.1 3.7 gather_fusion.1
  30.8 26.2 %copy.105 = bf16[16,2,196,512]{3,1,2,0:T(2,128)(2,1)} copy(bf16[16,2,196,512]{3,2,1,0:T(8,128)(2,1)} %bitcast.85) | data formatting | bytes 12845056 | tf_op jit(solution)/shard_map/gather | solution.py:78
  56.9 7.2 all-to-all-start.1
  72.4 3.5 copy.119
  76.6 102.4 %all-gather.2.cloned.1.call-done = bf16[2048,512]{1,0:T(8,128)(2,1)} async-done(((bf16[16,512]{1,0:T(8,128)(2,1)}), bf16[2048,512]{1,0:T(8,128)(2,1)}) %all-gather.2.cloned.1.call-update) | async-done | bytes 2097168 | tf_op jit(solution)/shard_map/all_gather | solution.py:115
  184.2 6.8 copy.106
  191.0 6.3 broadcast_in_dim.36
  197.4 122.8 %while.18 = (s32[]{:T(128)}, f32[32,196,512]{2,1,0:T(8,128)}, f32[4,4,196,512]{3,2,1,0:T(8,128)}, f32[4,4,196,512]{3,2,1,0:T(8,128)}, s32[4,4,3]{1,0,2:T(4,128)S...) while((s32[]{:T(128)}, f32[32,196,512]{2,1,0:T(8,128)}, ...), condition=%wide.region_11.12_spmd, body=%wide.region_6.11_spmd.sunk | while | flops 1898786432 | bytes 86222232 | solution.py:95
  200.1 3.6 gather_fusion
  211.7 2.9 slice.32
  215.9 12.0 %scatter_fusion = f32[32,196,512]{2,1,0:T(8,128)} fusion(f32[32,196,512]{2,1,0:T(8,128)} %get-tuple-element.336, s32[12]{0:T(128)S(1)} %fusion.64, f32[12,196,512]{2,1,0:T(8,128)} %bitcast.79), kind=kCustom, calls=%fused_computation.2.clone.1 | custom fusion | flops 1204224 | bytes 14450736 | tf_op jit(solution)/shard_map/while/body/eval_jaxpr/scatter-add | solution.py:89
  230.6 3.6 gather_fusion
  246.4 12.2 %scatter_fusion = f32[32,196,512]{2,1,0:T(8,128)} fusion(f32[32,196,512]{2,1,0:T(8,128)} %get-tuple-element.336, s32[12]{0:T(128)S(1)} %fusion.64, f32[12,196,512]{2,1,0:T(8,128)} %bitcast.79), kind=kCustom, calls=%fused_computation.2.clone.1 | custom fusion | flops 1204224 | bytes 14450736 | tf_op jit(solution)/shard_map/while/body/eval_jaxpr/scatter-add | solution.py:89
  261.3 3.6 gather_fusion
  272.9 2.9 slice.32
  277.1 12.1 %scatter_fusion = f32[32,196,512]{2,1,0:T(8,128)} fusion(f32[32,196,512]{2,1,0:T(8,128)} %get-tuple-element.336, s32[12]{0:T(128)S(1)} %fusion.64, f32[12,196,512]{2,1,0:T(8,128)} %bitcast.79), kind=kCustom, calls=%fused_computation.2.clone.1 | custom fusion | flops 1204224 | bytes 14450736 | tf_op jit(solution)/shard_map/while/body/eval_jaxpr/scatter-add | solution.py:89
  292.0 3.6 gather_fusion
  307.9 12.2 %scatter_fusion = f32[32,196,512]{2,1,0:T(8,128)} fusion(f32[32,196,512]{2,1,0:T(8,128)} %get-tuple-element.336, s32[12]{0:T(128)S(1)} %fusion.64, f32[12,196,512]{2,1,0:T(8,128)} %bitcast.79), kind=kCustom, calls=%fused_computation.2.clone.1 | custom fusion | flops 1204224 | bytes 14450736 | tf_op jit(solution)/shard_map/while/body/eval_jaxpr/scatter-add | solution.py:89
  320.1 8.3 convert_element_type.75
  328.4 26.4 %copy.112 = bf16[16,2,196,512]{3,1,2,0:T(2,128)(2,1)} copy(bf16[16,2,196,512]{3,2,1,0:T(8,128)(2,1)} %bitcast.86) | data formatting | bytes 12845056 | tf_op jit(solution)/shard_map/reshape | solution.py:106
  354.8 6.2 all-to-all-start.2
  365.7 21.5 %fusion.34 = bf16[16,196,512]{2,0,1:T(8,128)(2,1)} fusion(bf16[16,196,512]{2,0,1:T(8,128)(2,1)S(1)} %copy-done.3, f32[16,196,512]{2,1,0:T(8,128)} %bitcast.89, f32[16,512]{1,0:T(8,128)S(1)} %multiply_multiply_fusion.1, f32[16,196]{0,1:T(8,128)S(1)} %copy-done.8), kind=kOutput, calls=%fused_computation.56 | output fusion | flops 17665600 | bytes 12890368 | tf_op jit(solution)/shard_map/mul | solution.py:54
  387.2 70.3 %all-to-all-done.2 = bf16[16,2,196,512]{3,1,2,0:T(2,128)(2,1)} async-done(((bf16[16,2,196,512]{3,1,2,0:T(2,128)(2,1)}), bf16[16,2,196,512]{3,1,2,0:T(2,128)(2,1)}, u32[]{:S(2)}, u32[]{:S(2)}) %all-to-all-start.2) | async-done | bytes 6422560 | tf_op jit(solution)/shard_map/all_to_all | solution.py:107
  457.5 9.5 %copy_convert_fusion = f32[16,2,196,512]{3,0,2,1:T(8,128)} fusion(bf16[16,2,196,512]{3,1,2,0:T(2,128)(2,1)} %all-to-all-done.2), kind=kLoop, calls=%fused_computation.59 | loop fusion | flops 3211264 | bytes 19267584 | tf_op jit(solution)/shard_map/convert_element_type | solution.py:109
  467.1 16.8 %copy.114 = f32[16,2,196,512]{3,2,1,0:T(8,128)} copy(f32[16,2,196,512]{3,0,2,1:T(8,128)} %copy_convert_fusion) | data formatting | bytes 25690112 | tf_op jit(solution)/shard_map/convert_element_type | solution.py:109
  483.8 371.5 %reduce-scatter.2.cloned.1.call-done = f32[16,512]{1,0:T(8,128)} async-done(((f32[2048,512]{1,0:T(8,128)}), f32[16,512]{1,0:T(8,128)}) %reduce-scatter.2.cloned.1.call-update) | async-done | bytes 32784 | tf_op jit(solution)/shard_map/reduce_scatter | solution.py:129
  857.1 6.4 bitcast_add_fusion
  863.6 29.9 %scatter_fusion.1 = f32[16,196,512]{2,1,0:T(8,128)} fusion(f32[16,196,512]{2,1,0:T(8,128)} %bitcast_add_fusion, s32[32]{0:T(128)S(1)} %copy-done.16, f32[32,196,512]{2,1,0:T(8,128)} %bitcast.84), kind=kCustom, calls=%fused_computation.3 | custom fusion | flops 3211264 | bytes 38535296 | tf_op jit(solution)/shard_map/scatter-add | solution.py:108
  893.5 21.8 %fusion.30 = bf16[16,196,512]{2,1,0:T(8,128)(2,1)S(1)} fusion(f32[16,196,512]{2,1,0:T(8,128)} %scatter_fusion.1, f32[16,196]{1,0:T(8,128)S(1)} %copy-done.12, bf16[16,196,512]{2,0,1:T(8,128)(2,1)S(1)} %copy-done.4), kind=kOutput, calls=%fused_computation.51 | output fusion | flops 14454335 | bytes 12857600 | tf_op jit(solution)/shard_map/mul | solution.py:54
  (171 shorter events, 80.0 us)
Async XLA Ops:
  9.2 17.6 %all-to-all-start = ((s32[16,1,2]{2,1,0:T(1,128)}), s32[16,1,2]{2,1,0:T(1,128)S(1)}, u32[]{:S(2)}, u32[]{:S(2)}) async-start(s32[16,1,2]{2,1,0:T(1,128)} %copy.102), calls=%async_computation | async-start | bytes 16384 | tf_op jit(solution)/shard_map/all_to_all | solution.py:77
  22.9 0.6 copy-start.11
  26.8 38.2 %copy-start.5 = (f32[16,512]{1,0:T(8,128)}, f32[16,512]{1,0:T(8,128)S(1)}, u32[]{:S(2)}) copy-start(f32[16,512]{1,0:T(8,128)S(1)} %get-tuple-element.259) | copy-start | bytes 98308
  26.8 4.0 copy-start.9
  56.9 127.3 %all-to-all-start.1 = ((bf16[16,2,196,512]{3,1,2,0:T(2,128)(2,1)}), bf16[16,2,196,512]{3,1,2,0:T(2,128)(2,1)}, u32[]{:S(2)}, u32[]{:S(2)}) async-start(bf16[16,2,196,512]{3,1,2,0:T(2,128)(2,1)} %copy.105), calls=%async_computation.1 | async-start | bytes 12845056 | tf_op jit(solution)/shard_map/all_to_all | solution.py:79
  64.2 114.9 %all-gather.2.cloned.1.call-start = ((), (), s32[]{:S(2)}) async-start(), calls=%async_computation.4 | async-start | bytes 2113536 | tf_op jit(solution)/shard_map/all_gather | solution.py:115
  64.9 0.6 copy-start.13
  66.2 789.1 %reduce-scatter.2.cloned.1.call-start = ((), (), s32[]{:S(2)}) async-start(), calls=%async_computation.5 | async-start | bytes 4227072 | tf_op jit(solution)/shard_map/reduce_scatter | solution.py:129
  69.9 6.0 copy-start.7
  197.4 1.7 copy-start
  203.6 3.1 copy-start.2
  215.9 12.1 %copy-start.1 = (bf16[4,4,196,512]{3,2,1,0:T(8,128)(2,1)S(1)}, bf16[4,4,196,512]{3,2,1,0:T(8,128)(2,1)}, u32[]{:S(2)}) copy-start(bf16[4,4,196,512]{3,2,1,0:T(8,128)(2,1)} %copy-done) | copy-start | bytes 9633796 | tf_op jit(solution)/shard_map/while
  227.9 1.7 copy-start
  234.2 3.1 copy-start.2
  246.4 12.2 %copy-start.1 = (bf16[4,4,196,512]{3,2,1,0:T(8,128)(2,1)S(1)}, bf16[4,4,196,512]{3,2,1,0:T(8,128)(2,1)}, u32[]{:S(2)}) copy-start(bf16[4,4,196,512]{3,2,1,0:T(8,128)(2,1)} %copy-done) | copy-start | bytes 9633796 | tf_op jit(solution)/shard_map/while
  258.6 1.7 copy-start
  264.9 3.1 copy-start.2
  277.1 12.2 %copy-start.1 = (bf16[4,4,196,512]{3,2,1,0:T(8,128)(2,1)S(1)}, bf16[4,4,196,512]{3,2,1,0:T(8,128)(2,1)}, u32[]{:S(2)}) copy-start(bf16[4,4,196,512]{3,2,1,0:T(8,128)(2,1)} %copy-done) | copy-start | bytes 9633796 | tf_op jit(solution)/shard_map/while
  289.3 1.7 copy-start
  295.6 3.1 copy-start.2
  307.9 12.2 %copy-start.1 = (bf16[4,4,196,512]{3,2,1,0:T(8,128)(2,1)S(1)}, bf16[4,4,196,512]{3,2,1,0:T(8,128)(2,1)}, u32[]{:S(2)}) copy-start(bf16[4,4,196,512]{3,2,1,0:T(8,128)(2,1)} %copy-done) | copy-start | bytes 9633796 | tf_op jit(solution)/shard_map/while
  354.8 6.8 copy-start.10
  354.8 10.9 %copy-start.3 = (bf16[16,196,512]{2,0,1:T(8,128)(2,1)S(1)}, bf16[16,196,512]{2,0,1:T(8,128)(2,1)}, u32[]{:S(2)}) copy-start(bf16[16,196,512]{2,0,1:T(8,128)(2,1)} %param.5) | copy-start | bytes 9633796
  354.8 10.9 %copy-start.8 = (f32[16,196]{0,1:T(8,128)S(1)}, f32[16,196]{0,1:T(8,128)}, u32[]{:S(2)}) copy-start(f32[16,196]{0,1:T(8,128)} %copy-done.7) | copy-start | bytes 37636
  354.8 102.7 %all-to-all-start.2 = ((bf16[16,2,196,512]{3,1,2,0:T(2,128)(2,1)}), bf16[16,2,196,512]{3,1,2,0:T(2,128)(2,1)}, u32[]{:S(2)}, u32[]{:S(2)}) async-start(bf16[16,2,196,512]{3,1,2,0:T(2,128)(2,1)} %copy.112), calls=%async_computation.3 | async-start | bytes 12845056 | tf_op jit(solution)/shard_map/all_to_all | solution.py:107
  467.0 388.3 %copy-start.6 = (f32[16,512]{1,0:T(8,128)S(1)}, f32[16,512]{1,0:T(8,128)}, u32[]{:S(2)}) copy-start(f32[16,512]{1,0:T(8,128)} %copy-done.5) | copy-start | bytes 98308
  467.0 388.3 %copy-start.14 = (f32[16]{0:T(128)S(1)}, f32[16]{0:T(128)}, u32[]{:S(2)}) copy-start(f32[16]{0:T(128)} %copy-done.13) | copy-start | bytes 196
  467.1 389.2 %copy-start.15 = (f32[16]{0:T(128)S(1)}, f32[16]{0:T(128)}, u32[]{:S(2)}) copy-start(f32[16]{0:T(128)} %get-tuple-element.261) | copy-start | bytes 196
  857.1 6.4 copy-start.16
  863.6 29.9 %copy-start.4 = (bf16[16,196,512]{2,0,1:T(8,128)(2,1)S(1)}, bf16[16,196,512]{2,0,1:T(8,128)(2,1)}, u32[]{:S(2)}) copy-start(bf16[16,196,512]{2,0,1:T(8,128)(2,1)} %param.6) | copy-start | bytes 9633796
  863.6 29.9 %copy-start.12 = (f32[16,196]{1,0:T(8,128)S(1)}, f32[16,196]{1,0:T(8,128)}, u32[]{:S(2)}) copy-start(f32[16,196]{1,0:T(8,128)} %copy-done.11) | copy-start | bytes 37636
Sparse Core Ops, SparseCore 0:
  68.6 110.4 all-gather.1
  184.3 670.9 reduce-scatter.1
where the time goes:
time: 936 us; the launch traced here: 925 us
  waiting for transfers between devices  544 us (58%)
  other arithmetic  168 us (18%)
  local copies, waits for them, and re-layouts  138 us (15%)
  matrix products  38.2 us (4%)
  starting transfers between devices  22 us (2%)
  between operations  14.4 us (2%)
    reduce_scatter x1, waiting for transfers between devices, per_device(): lax.psum_scatter(lax.dot_general(nce_coef, sar_pool_bf, (((0,), (0,)), ((...  372 us
    all_gather x1, waiting for transfers between devices, per_device(): opt_all = lax.all_gather(opt_pool_bf, ('sar', 'opt'), axis=0, tiled=True)  102 us
    all_to_all x1, waiting for transfers between devices, per_device(): lax.all_to_all(slot_round, 'opt', split_axis=0, concat_axis=0, tiled=True)  70.3 us
    scatter-add x4, other arithmetic, pair_step(): slot_sums.at[slot_rows.reshape(-1)]  48.6 us
    mul x2, other arithmetic, finish(): unit_tokens * jnp.sum(unit_tokens * total, axis=-1, keepdims=True)  43.4 us
    gather x2, local copies, waits for them, and re-layouts, per_device(): rows = opt_bf[asked]  29.9 us
    scatter-add x1, other arithmetic, per_device(): own_pair.at[asked.reshape(-1)]  29.9 us
    reshape x1, local copies, waits for them, and re-layouts, per_device(): slot_sums.astype(jnp.bfloat16).reshape(groups, CAP, length, width)  26.4 us
  transfers between devices with their start and end apart: 5, of which 3 were waited for; matrix products, arithmetic and copies ran while one was open for 26% of the time, Pallas kernels for 0%

commit v1 on v0

v1 whole, which is shorter than its diff:
```python
import functools

import jax
import jax.numpy as jnp
from jax import lax
from jax.experimental import pallas as pl
from jax.experimental.pallas import tpu as pltpu
from jax.sharding import PartitionSpec as P

NEG = 3
CAP = 2
EPSILON = 1e-06
POOL_TEMP = 0.02
CAND_TEMP = 0.1
NCE_TEMP = 0.07
LOSS_SCALE = 256.0
NCE_SCALE = 0.05 * 256.0 / 0.07
LOG2E = 1.4426950408889634

T = 16
L = 196
D = 512
MAIN = 192
ROWS = 208
LANES = 256
PAIRS = T * NEG
GROUPS = 16
SIDE = 4
SLOTS = (GROUPS - 1) * CAP
CHUNK = 48
CHUNKS = MAIN // CHUNK
HALF = D // 2
FIRST = 3 * CHUNK
ORDER = [10, 2, 8, 6, 14, 9, 11, 5, 7, 13, 15, 1, 3, 4, 12]

SLOT_AT, PAIR_AT, TILE_AT, SAME_AT, LAST_AT, TABLE = 0, 48, 96, 144, 192, 256

BF16 = jnp.bfloat16
F32 = jnp.float32


def negated(turn):
    return ((SIDE - turn // SIDE) % SIDE) * SIDE + (SIDE - turn % SIDE) % SIDE


def dot(a, b, dims):
    return lax.dot_general(a, b, (dims, ((), ())), preferred_element_type=F32)


NN, NT, TN = ((1,), (0,)), ((1,), (1,)), ((0,), (0,))


def inverse_norm(rows):
    return lax.rsqrt(jnp.sum(rows * rows, axis=-1, keepdims=True) + EPSILON)


def finish_rows(raw, back, pair):
    inverse = inverse_norm(raw)
    unit = raw * inverse
    total = pair + back
    return ((total - unit * jnp.sum(unit * total, axis=-1, keepdims=True)) * inverse).astype(BF16)


def kernel(
    n_sar, table, ids, sar_raw, opt_raw, sar_out, opt_out,
    sar_rows, opt_rows, outbox, out_tail, fetched, fetched_end, fetched_tail, weight, parts, acc,
    returned, returned_tail, tail_sums, pools, sums, own_pair, means, pool_rows, backs, totals,
    scale, tail_buf, ids_in, ids_smem, keys, ranks, order2, same2, last2,
    ids_send, ids_recv, ids_sem, fetch_send, fetch_recv, back_send, back_recv,
    plane_send, plane_recv, block_send, block_recv, write_sem,
):
    my_sar = lax.axis_index("sar")
    me = lax.axis_index("opt")
    my_z, my_x = me // SIDE, me % SIDE

    def peer(turn):
        z = (my_z + turn // SIDE) % SIDE
        x = (my_x + turn % SIDE) % SIDE
        return {"opt": z * SIDE + x}

    def sar_peer(step):
        return {"sar": (my_sar + step) % n_sar}

    def remote(src, dst, send, recv, to):
        return pltpu.make_async_remote_copy(
            src_ref=src, dst_ref=dst, send_sem=send, recv_sem=recv,
            device_id=to, device_id_type=pl.DeviceIdType.MESH,
        )

    barrier = pltpu.get_barrier_semaphore()
    for turn in range(1, GROUPS):
        pl.semaphore_signal(
            barrier, inc=1, device_id=peer(turn), device_id_type=pl.DeviceIdType.MESH
        )
    for step in range(1, n_sar):
        pl.semaphore_signal(
            barrier, inc=1, device_id=sar_peer(step), device_id_type=pl.DeviceIdType.MESH
        )

    tail_buf[...] = jnp.zeros_like(tail_buf)

    def normalize(which, raw, rows):
        def tile(i, carry):
            main = raw[i, 0:MAIN].astype(F32)
            tail_buf[0:4] = raw[i, MAIN:L].astype(F32)
            tail = tail_buf[...]
            unit = main * inverse_norm(main)
            unit_tail = tail * inverse_norm(tail)
            rows[i, 0:MAIN] = unit.astype(BF16)
            rows[i, MAIN:ROWS] = unit_tail.astype(BF16)
            mean = (
                jnp.sum(unit, axis=0, keepdims=True) + jnp.sum(unit_tail, axis=0, keepdims=True)
            ) * (1.0 / L)
            means[which, pl.ds(i, 1), :] = mean
            return carry

        lax.fori_loop(0, T, tile, 0)

    normalize(1, opt_raw, opt_rows)

    pl.semaphore_wait(barrier, GROUPS - 1 + n_sar - 1)

    def ids_copy(turn):
        return remote(
            ids.at[turn], ids_in.at[turn], ids_send.at[turn], ids_recv.at[turn], peer(turn)
        )

    for turn in ORDER:
        ids_copy(turn).start()
    for turn in ORDER:
        ids_copy(turn).wait()
    to_smem = pltpu.make_async_copy(ids_in, ids_smem, ids_sem)
    to_smem.start()
    to_smem.wait()

    def fetch_copy(turn, c):
        box = pl.ds((turn - 1) * CAP, CAP)
        if c == CHUNKS:
            src, dst = out_tail.at[turn - 1], fetched_tail.at[turn - 1]
        else:
            at = pl.ds(c * CHUNK, CHUNK)
            src = outbox.at[box, at]
            if c * CHUNK < FIRST:
                dst = fetched.at[box, at]
            else:
                dst = fetched_end.at[box, pl.ds(c * CHUNK - FIRST, CHUNK)]
        return remote(src, dst, fetch_send.at[turn, c], fetch_recv.at[turn, c], peer(turn))

    for c in range(CHUNKS + 1):
        for turn in ORDER:
            asker = negated(turn)
            if c < CHUNKS:
                for s in range(CAP):
                    outbox[(turn - 1) * CAP + s, c * CHUNK : (c + 1) * CHUNK] = opt_rows[
                        ids_smem[asker, 0, s], c * CHUNK : (c + 1) * CHUNK
                    ]
            else:
                ends = [
                    opt_rows[ids_smem[asker, 0, s], MAIN:ROWS].astype(F32)[0:8] for s in range(CAP)
                ]
                out_tail[turn - 1] = jnp.concatenate(ends, axis=0).astype(BF16)
            fetch_copy(turn, c).start()

    def clear(i, carry):
        sar_rows[i, ROWS:LANES] = jnp.zeros((LANES - ROWS, D), BF16)
        return carry

    lax.fori_loop(0, T, clear, 0)
    normalize(0, sar_raw, sar_rows)

    mine = pl.ds(pl.multiple_of(me * T, T), T)
    for which in range(2):
        mean = means[which]
        pool_scale = lax.rsqrt(jnp.sum(mean * mean, axis=-1, keepdims=True) + EPSILON)
        pool = mean * pool_scale
        pool_rows[which] = pool
        pools[my_sar, which, mine, :] = pool.astype(BF16)

    def plane_copy(turn):
        here = pools.at[my_sar, :, mine, :]
        return remote(here, here, plane_send.at[turn], plane_recv.at[turn], peer(turn))

    for turn in ORDER:
        plane_copy(turn).start()

    def exp_scores(rows, i):
        return jnp.exp2(dot(rows, sar_rows[i], NT) * (LOG2E / POOL_TEMP))

    live = lax.broadcasted_iota(jnp.int32, (ROWS, LANES), 0) < L

    def own_scores(i, carry):
        e = exp_scores(opt_rows[i], i)
        weight[i] = e.astype(BF16)
        totals[0, pl.ds(i, 1), :] = jnp.sum(jnp.where(live, e, 0.0), axis=0, keepdims=True)
        return carry

    lax.fori_loop(0, T, own_scores, 0)

    for p in range(SLOTS):
        keys[p] = ids_smem[p // CAP + 1, 0, p % CAP] * 32 + p

    def rank_of(p, carry):
        key = keys[p]
        rank = jnp.int32(0)
        for q in range(SLOTS):
            rank += (keys[q] < key).astype(jnp.int32)
        ranks[p] = rank
        return carry

    lax.fori_loop(0, SLOTS, rank_of, 0)

    def place_of(t, before):
        key = jnp.int32(0)
        for p in range(SLOTS):
            key += jnp.where(ranks[p] == t, keys[p], 0)
        tile = key // 32
        order2[t] = key % 32
        same2[t] = (tile == before).astype(jnp.int32)
        return tile

    lax.fori_loop(0, SLOTS, place_of, jnp.int32(-1))

    def last_of(j, before):
        upto = jnp.int32(0)
        for p in range(SLOTS):
            upto += (keys[p] < (j + 1) * 32).astype(jnp.int32)
        last2[j] = jnp.where(upto > before, upto - 1, SLOTS)
        return upto

    lax.fori_loop(0, T, last_of, jnp.int32(0))

    for turn in ORDER:
        plane_copy(turn).wait_recv()

    def block_copy(step):
        here = pools.at[my_sar]
        return remote(here, here, block_send.at[step], block_recv.at[step], sar_peer(step))

    for step in range(1, n_sar):
        block_copy(step).start()

    for c in range(FIRST // CHUNK):
        for turn in ORDER:
            fetch_copy(turn, c).wait_recv()

    def first_scores(i, carry):
        for k in range(NEG):
            e = exp_scores(fetched[table[SLOT_AT + i * NEG + k]], i)
            weight[T + i * NEG + k, 0:FIRST] = e.astype(BF16)
            totals[k + 1, pl.ds(i, 1), :] = jnp.sum(e, axis=0, keepdims=True)
        return carry

    lax.fori_loop(0, T, first_scores, 0)

    for c in range(FIRST // CHUNK, CHUNKS + 1):
        for turn in ORDER:
            fetch_copy(turn, c).wait_recv()
    for turn in range(1, GROUPS):
        ends = fetched_tail[turn - 1].astype(F32)
        for s in range(CAP):
            end = ends[8 * s : 8 * s + 8]
            fetched_end[(turn - 1) * CAP + s, MAIN - FIRST :] = jnp.concatenate(
                [end, jnp.zeros_like(end)], axis=0
            ).astype(BF16)

    live_end = lax.broadcasted_iota(jnp.int32, (ROWS - FIRST, LANES), 0) < L - FIRST

    def last_scores(i, carry):
        for k in range(NEG):
            e = exp_scores(fetched_end[table[SLOT_AT + i * NEG + k]], i)
            weight[T + i * NEG + k, FIRST:ROWS] = e.astype(BF16)
            totals[k + 1, pl.ds(i, 1), :] += jnp.sum(
                jnp.where(live_end, e, 0.0), axis=0, keepdims=True
            )
        return carry

    lax.fori_loop(0, T, last_scores, 0)

    tokens = lax.broadcasted_iota(jnp.int32, (T, LANES), 1) < L
    cand = []
    for k in range(NEG + 1):
        logs = jnp.where(tokens, jnp.log(totals[k]), 0.0)
        match = (POOL_TEMP / L) * jnp.sum(logs, axis=-1, keepdims=True)
        cand.append(jnp.exp(match / CAND_TEMP))
    cand_sum = cand[0] + cand[1] + cand[2] + cand[3]
    for k in range(NEG + 1):
        coef = LOSS_SCALE * (cand[k] / cand_sum - (1.0 if k == 0 else 0.0)) / CAND_TEMP
        scaled = (coef / L) / totals[k]
        for i in range(T):
            scale[i if k == 0 else T + i * NEG + k - 1] = scaled[i : i + 1]

    def weights(p):
        return (weight[p].astype(F32) * scale[p]).astype(BF16)

    def back_copy(turn, h, c):
        box = pl.ds((turn - 1) * CAP, CAP)
        if c is None:
            src, dst = out_tail.at[turn - 1], returned_tail.at[turn - 1]
            sem = 2 * CHUNKS
        else:
            at, cols = pl.ds(c * CHUNK, CHUNK), pl.ds(h * HALF, HALF)
            src, dst = outbox.at[box, at, cols], returned[c].at[box, :, cols]
            sem = h * CHUNKS + c
        return remote(src, dst, back_send.at[turn, sem], back_recv.at[turn, sem], peer(turn))

    parts[PAIRS] = jnp.zeros((ROWS, HALF), BF16)
    for c in range(CHUNKS + 1):
        for turn in ORDER:
            fetch_copy(turn, c).wait_send()
    for h in range(2):
        cols = slice(h * HALF, (h + 1) * HALF)
        acc[...] = jnp.zeros_like(acc)

        def add_pair(p, carry, cols=cols):
            pair = table[PAIR_AT + p]
            keep = table[SAME_AT + p].astype(F32)
            part = dot(weights(T + pair), sar_rows[table[TILE_AT + p], :, cols], NN)
            total = acc[...] * keep + part
            acc[...] = total
            parts[p] = total.astype(BF16)
            return carry

        lax.fori_loop(0, PAIRS, add_pair, 0)

        for c in range(CHUNKS):
            at = slice(c * CHUNK, (c + 1) * CHUNK)
            for turn in ORDER:
                for s in range(CAP):
                    last = table[LAST_AT + (negated(turn) - 1) * CAP + s]
                    outbox[(turn - 1) * CAP + s, at, cols] = parts[last, at, :]
                back_copy(turn, h, c).start()
        for turn in ORDER:
            ends = [
                parts[table[LAST_AT + (negated(turn) - 1) * CAP + s], MAIN:ROWS].astype(F32)[0:8]
                for s in range(CAP)
            ]
            out_tail[turn - 1, :, cols] = jnp.concatenate(ends, axis=0).astype(BF16)
            if h:
                back_copy(turn, h, None).start()

    for step in range(1, n_sar):
        block_copy(step).wait_recv()
    block = pools.shape[2]
    logit_scale = LOG2E / NCE_TEMP
    own_sar = pools[my_sar, 0, mine, :]
    own_opt = pools[my_sar, 1, mine, :]

    def own_rows(t, row_sums):
        e = jnp.exp2(dot(own_sar, pools[t, 1], NT) * logit_scale)
        return row_sums + jnp.sum(e, axis=-1, keepdims=True)

    row_sums = lax.fori_loop(0, n_sar, own_rows, jnp.zeros((T, 1), F32))

    def own_coefs(t, grad):
        e = jnp.exp2(dot(own_sar, pools[t, 1], NT) * logit_scale)
        rows = my_sar * block + me * T + lax.broadcasted_iota(jnp.int32, (T, block), 0)
        columns = t * block + lax.broadcasted_iota(jnp.int32, (T, block), 1)
        diagonal = (rows == columns).astype(F32)
        coefs = (NCE_SCALE * (e / row_sums - diagonal)).astype(BF16)
        return grad + dot(coefs, pools[t, 1], NN)

    sar_pool_grad = lax.fori_loop(0, n_sar, own_coefs, jnp.zeros((T, D), F32))

    def opt_coefs(s, grad):
        rows_here = pools[s, 0]

        def add_sums(t, sums_here):
            e = jnp.exp2(dot(rows_here, pools[t, 1], NT) * logit_scale)
            return sums_here + jnp.sum(e, axis=-1, keepdims=True)

        sums_here = lax.fori_loop(0, n_sar, add_sums, jnp.zeros((block, 1), F32))
        e = jnp.exp2(dot(rows_here, own_opt, NT) * logit_scale)
        rows = s * block + lax.broadcasted_iota(jnp.int32, (block, T), 0)
        columns = my_sar * block + me * T + lax.broadcasted_iota(jnp.int32, (block, T), 1)
        diagonal = (rows == columns).astype(F32)
        coefs = (NCE_SCALE * (e / sums_here - diagonal)).astype(BF16)
        return grad + dot(coefs, rows_here, TN)

    opt_pool_grad = lax.fori_loop(0, n_sar, opt_coefs, jnp.zeros((T, D), F32))

    for which, grad in enumerate((sar_pool_grad, opt_pool_grad)):
        mean = means[which]
        pool_scale = lax.rsqrt(jnp.sum(mean * mean, axis=-1, keepdims=True) + EPSILON)
        pool = pool_rows[which]
        along = jnp.sum(pool * grad, axis=-1, keepdims=True)
        backs[which] = (grad - pool * along) * pool_scale * (1.0 / L)

    def raw_tail(raw, i):
        tail_buf[0:4] = raw[i, MAIN:L].astype(F32)
        return tail_buf[...]

    def sar_tile(i, carry):
        own = weights(i)
        own_pair[i] = dot(own, sar_rows[i], NN)
        cands = [opt_rows[i]]
        coefs = [own]
        for k in range(NEG):
            cands.append(fetched[table[SLOT_AT + i * NEG + k]])
            cands.append(fetched_end[table[SLOT_AT + i * NEG + k]])
            coefs.append(weights(T + i * NEG + k))
        pair = dot(jnp.concatenate(coefs, axis=0), jnp.concatenate(cands, axis=0), TN)
        back = backs[0, pl.ds(i, 1), :]
        opt_rows[i, 0:MAIN] = finish_rows(sar_raw[i, 0:MAIN].astype(F32), back, pair[0:MAIN])
        opt_rows[i, MAIN:ROWS] = finish_rows(raw_tail(sar_raw, i), back, pair[MAIN:ROWS])
        return carry

    lax.fori_loop(0, T, sar_tile, 0)
    write_sar = pltpu.make_async_copy(opt_rows, sar_out, write_sem.at[CHUNKS + 1])
    write_sar.start()

    sums[SLOTS] = jnp.zeros((CHUNK, D), F32)
    tail_sums[SLOTS] = jnp.zeros((8, D), F32)
    writes = []
    for c in range(CHUNKS):
        at = slice(c * CHUNK, (c + 1) * CHUNK)
        for turn in ORDER:
            back_copy(turn, 0, c).wait_recv()
            back_copy(turn, 1, c).wait_recv()

        def add_slot(t, total, c=c):
            total = total * same2[t].astype(F32) + returned[c][order2[t]].astype(F32)
            sums[t] = total
            return total

        lax.fori_loop(0, SLOTS, add_slot, jnp.zeros((CHUNK, D), F32))

        if c * CHUNK < FIRST:
            stage, stage_at = fetched, c * CHUNK
        else:
            stage, stage_at = fetched_end, c * CHUNK - FIRST

        def opt_tile(j, carry, at=at, stage=stage, stage_at=stage_at):
            pair = own_pair[j, at] + sums[last2[j]]
            stage[j, stage_at : stage_at + CHUNK] = finish_rows(
                opt_raw[j, at].astype(F32), backs[1, pl.ds(j, 1), :], pair
            )
            return carry

        lax.fori_loop(0, T, opt_tile, 0)
        rows_at = pl.ds(c * CHUNK, CHUNK)
        write = pltpu.make_async_copy(
            stage.at[pl.ds(0, T), pl.ds(stage_at, CHUNK)], opt_out.at[:, rows_at], write_sem.at[c]
        )
        write.start()
        writes.append(write)

    for turn in ORDER:
        back_copy(turn, 1, None).wait_recv()

    def add_tail(t, total):
        place = order2[t]
        both = returned_tail[place // CAP].astype(F32)
        second = (place % CAP).astype(F32)
        total = total * same2[t].astype(F32) + both[0:8] * (1.0 - second) + both[8:16] * second
        tail_sums[t] = total
        return total

    lax.fori_loop(0, SLOTS, add_tail, jnp.zeros((8, D), F32))

    def opt_tail(j, carry):
        part = tail_sums[last2[j]]
        pair = own_pair[j, MAIN:ROWS] + jnp.concatenate([part, jnp.zeros_like(part)], axis=0)
        fetched_end[j, MAIN - FIRST :] = finish_rows(raw_tail(opt_raw, j), backs[1, pl.ds(j, 1), :], pair)
        return carry

    lax.fori_loop(0, T, opt_tail, 0)
    rows_at = pl.ds(MAIN, ROWS - MAIN)
    write = pltpu.make_async_copy(
        fetched_end.at[pl.ds(0, T), pl.ds(MAIN - FIRST, ROWS - MAIN)],
        opt_out.at[:, rows_at],
        write_sem.at[CHUNKS],
    )
    write.start()
    writes.append(write)

    for turn in ORDER:
        plane_copy(turn).wait_send()
        for c in range(CHUNKS):
            back_copy(turn, 0, c).wait_send()
            back_copy(turn, 1, c).wait_send()
        back_copy(turn, 1, None).wait_send()
    for step in range(1, n_sar):
        block_copy(step).wait_send()
    write_sar.wait()
    for write in writes:
        write.wait()


def index_tables(candidates):
    me = lax.axis_index("opt")
    block = T * GROUPS
    local_ids = (candidates % block).reshape(-1)
    hits = (local_ids[:, None] == jnp.arange(block)[None, :]).astype(jnp.int32)
    needed = jnp.max(hits, axis=0).reshape(GROUPS, T)
    rank = jnp.cumsum(needed, axis=1) - needed
    chosen = needed[:, :, None] * (rank[:, :, None] == jnp.arange(CAP)[None, None, :])
    asked = jnp.sum(chosen * jnp.arange(T)[None, :, None], axis=1)
    pair_rank = jnp.sum(hits * rank.reshape(-1)[None, :], axis=1)
    owner = local_ids // T
    turn = ((me // SIDE - owner // SIDE) % SIDE) * SIDE + (me % SIDE - owner % SIDE) % SIDE
    slot = (turn - 1) * CAP + pair_rank
    turns = jnp.arange(GROUPS)
    owners = ((me // SIDE + turns // SIDE) % SIDE) * SIDE + (me % SIDE + turns % SIDE) % SIDE
    by_turn = jnp.sum(
        (owners[:, None] == jnp.arange(GROUPS)[None, :])[:, :, None] * asked[None], axis=1
    )
    ids = jnp.zeros((GROUPS, 1, 128), jnp.int32).at[:, 0, :CAP].set(by_turn)
    pairs = jnp.arange(PAIRS)
    key = slot * 64 + pairs
    place = jnp.sum(key[None, :] < key[:, None], axis=1)
    at_place = place[None, :] == pairs[:, None]
    sorted_key = jnp.sum(at_place * key[None, :], axis=1)
    sorted_pair, sorted_slot = sorted_key % 64, sorted_key // 64
    same = (sorted_slot == jnp.concatenate([jnp.full((1,), -1), sorted_slot[:-1]])).astype(jnp.int32)
    slots = jnp.arange(SLOTS)
    upto = jnp.sum(slot[None, :] <= slots[:, None], axis=1)
    used = jnp.any(slot[None, :] == slots[:, None], axis=1)
    last = jnp.where(used, upto - 1, PAIRS)
    table = jnp.concatenate(
        [slot, sorted_pair, sorted_pair // NEG, same, last, jnp.zeros((TABLE - LAST_AT - SLOTS,))]
    )
    return table.astype(jnp.int32), ids


def per_device(n_sar, sar_tokens, opt_tokens, candidates):
    table, ids = index_tables(candidates)
    vmem = pl.BlockSpec(memory_space=pltpu.VMEM)
    dma = pltpu.SemaphoreType.DMA
    padded = jax.ShapeDtypeStruct((T, ROWS, D), BF16)
    grads = pl.pallas_call(
        functools.partial(kernel, n_sar),
        out_shape=(padded, padded),
        in_specs=[pl.BlockSpec(memory_space=pltpu.SMEM), vmem, vmem, vmem],
        out_specs=[pl.BlockSpec(memory_space=pl.ANY)] * 2,
        scratch_shapes=[
            pltpu.VMEM((T, LANES, D), BF16),
            pltpu.VMEM((T, ROWS, D), BF16),
            pltpu.VMEM((SLOTS, MAIN, D), BF16),
            pltpu.VMEM((GROUPS - 1, 16, D), BF16),
            pltpu.VMEM((SLOTS, FIRST, D), BF16),
            pltpu.VMEM((SLOTS, ROWS - FIRST, D), BF16),
            pltpu.VMEM((GROUPS - 1, 16, D), BF16),
            pltpu.VMEM((T + PAIRS, ROWS, LANES), BF16),
            pltpu.VMEM((PAIRS + 1, ROWS, HALF), BF16),
            pltpu.VMEM((ROWS, HALF), F32),
            [pltpu.VMEM((SLOTS, CHUNK, D), BF16)] * CHUNKS,
            pltpu.VMEM((GROUPS - 1, 16, D), BF16),
            pltpu.VMEM((SLOTS + 1, 8, D), F32),
            pltpu.VMEM((n_sar, 2, T * GROUPS, D), BF16),
            pltpu.VMEM((SLOTS + 1, CHUNK, D), F32),
            pltpu.VMEM((T, ROWS, D), F32),
            pltpu.VMEM((2, T, D), F32),
            pltpu.VMEM((2, T, D), F32),
            pltpu.VMEM((2, T, D), F32),
            pltpu.VMEM((NEG + 1, T, LANES), F32),
            pltpu.VMEM((T + PAIRS, 1, LANES), F32),
            pltpu.VMEM((16, D), F32),
            pltpu.VMEM((GROUPS, 1, 128), jnp.int32),
            pltpu.SMEM((GROUPS, 1, 128), jnp.int32),
            pltpu.SMEM((32,), jnp.int32),
            pltpu.SMEM((32,), jnp.int32),
            pltpu.SMEM((32,), jnp.int32),
            pltpu.SMEM((32,), jnp.int32),
            pltpu.SMEM((32,), jnp.int32),
            dma((GROUPS,)),
            dma((GROUPS,)),
            dma,
            dma((GROUPS, CHUNKS + 1)),
            dma((GROUPS, CHUNKS + 1)),
            dma((GROUPS, 2 * CHUNKS + 1)),
            dma((GROUPS, 2 * CHUNKS + 1)),
            dma((GROUPS,)),
            dma((GROUPS,)),
            dma((n_sar,)),
            dma((n_sar,)),
            dma((CHUNKS + 2,)),
        ],
        compiler_params=pltpu.CompilerParams(
            collective_id=0, has_side_effects=True, vmem_limit_bytes=63 * 2**20
        ),
        name="match_grads",
    )(table, ids, sar_tokens, opt_tokens)
    return tuple(grad[:, :L] for grad in grads)


def solution(mesh):
    tiles = P(("sar", "opt"), None, None)
    return jax.shard_map(
        functools.partial(per_device, mesh.shape["sar"]),
        mesh=mesh,
        in_specs=(tiles, tiles, P(("sar", "opt"), None)),
        out_specs=(tiles, tiles),
        check_vma=False,
    )
```

time: 936 us -> 235 us (0.25)
  waiting for transfers between devices: 544 us -> 0 us
  Pallas kernels: 0 us -> 209 us
  other arithmetic: 168 us -> 2.7 us
  local copies, waits for them, and re-layouts: 138 us -> 18.1 us
  matrix products: 38.2 us -> 0 us
  starting transfers between devices: 22 us -> 0 us
  between operations: 14.4 us -> 0.77 us
    reduce_scatter x1 -> x0, waiting for transfers between devices: 372 us -> none  [per_device(): lax.psum_scatter(lax.dot_general(nce_coef, sar_pool_bf, (((0,), (0,)), ((...]
    pallas_call x0 -> x1, Pallas kernels: none -> 209 us  [per_device(): pl.pallas_call(functools.partial(kernel, n_sar), out_shape=(padded, padde...]
    all_gather x1 -> x0, waiting for transfers between devices: 102 us -> none  [per_device(): opt_all = lax.all_gather(opt_pool_bf, ('sar', 'opt'), axis=0, tiled=True)]
    scatter-add x5 -> x0, other arithmetic: 78.5 us -> none  [the longest x4 48.6 us: pair_step(): slot_sums.at[slot_rows.reshape(-1)]]
    all_to_all x3 -> x0, waiting for transfers between devices: 70.3 us -> none  [the longest x1 70.3 us: per_device(): lax.all_to_all(slot_round, 'opt', split_axis=0, concat_axis=0, tiled=True)]
    gather x6 -> x0, local copies, waits for them, and re-layouts: 44.2 us -> none  [the longest x2 29.9 us: per_device(): rows = opt_bf[asked]]
    mul x3 -> x0, other arithmetic: 43.4 us -> none  [the longest x2 43.4 us: finish(): unit_tokens * jnp.sum(unit_tokens * total, axis=-1, keepdims=True)]
    dot_general x15 -> x0, matrix products: 38.2 us -> none  [the longest x4 11.1 us: pair_grads(): jnp.einsum('kab,kbd->ad', weights, cand_rows, preferred_element_type=jnp....]
  transfers between devices with their start and end apart: 5 -> 0, of which waited for: 3 -> 0; matrix products, arithmetic and copies ran while one was open for 26% -> 0% of each run, Pallas kernels for 0% -> 0%
where the time goes in v1:
time: 235 us; the launch traced here: 230 us
  Pallas kernels  209 us (89%)
  local copies, waits for them, and re-layouts  18.1 us (8%)
  other arithmetic  2.7 us (1%)
    pallas_call x1, Pallas kernels, per_device(): pl.pallas_call(functools.partial(kernel, n_sar), out_shape=(padded, padde...  209 us
    unnamed x8, local copies, waits for them, and re-layouts  14.6 us

profile of v1, /device:TPU:2, one launch (start us, length us, event | category | flops | bytes accessed | tf_op | source)
XLA Modules:
  0.0 230.2 jit_solution(16316365155023444664)
XLA Ops:
  0.7 0.7 add_select_fusion
  1.4 0.1 copy.17
  1.4 0.1 reshape.325
  1.5 0.1 convert_reduce_fusion
  1.6 0.1 fusion.1
  1.7 0.1 reshape.326
  1.8 0.2 reduce_window_sum.13
  2.0 0.1 reduce_window_sum.14
  2.0 0.2 select_reduce_fusion
  2.3 0.1 multiply_reduce_fusion.1
  2.4 0.1 multiply_reduce_fusion
  2.5 0.0 copy-start
  2.5 0.2 convert_reduce_fusion.1
  2.7 0.1 select_reduce_fusion.1
  2.8 0.1 fusion
  2.9 0.1 convert_reduce_fusion.2
  3.1 0.1 fusion.9
  3.2 0.1 concatenate.9
  3.3 0.6 convert_element_type.49.table
  3.9 0.1 copy.18
  3.9 0.6 scatter.4.ids
  4.5 5.4 %copy.19.sar_raw = bf16[16,196,512]{2,1,0:T(8,128)(2,1)} copy(bf16[16,196,512]{2,0,1:T(8,128)(2,1)} %param.5) | data formatting | bytes 6422528 | tf_op args[0]
  10.0 0.0 copy-done
  10.0 3.6 %copy.20.opt_raw = bf16[16,196,512]{2,1,0:T(8,128)(2,1)} copy(bf16[16,196,512]{2,0,1:T(8,128)(2,1)S(1)} %copy-done) | data formatting | bytes 6422528 | tf_op args[1]
  13.5 208.6 %match_grads.1 = (bf16[16,208,512]{2,1,0:T(8,128)(2,1)}, bf16[16,208,512]{2,1,0:T(8,128)(2,1)}) custom-call(s32[256]{0:T(256)} %convert_element_type.49.table, s32[16,1,128]{2,1,0:T(1,128)} %scatter.4.ids, bf16[16,196,512]{2,1,0:T(8,128)(2,1)} %copy.19.sar_raw, bf16[16,196,512]{2,1,0:T(8,128)(2,1)} %copy.20.opt_raw), custom_call_target="tpu_custom_call" | custom-call | tf_op jit(solution)/shard_map/match_grads/pallas_call | solution.py:530
  222.1 2.1 slice.33
  224.3 0.0 copy-start.1
  224.3 2.8 %copy.21 = bf16[16,196,512]{2,0,1:T(8,128)(2,1)} copy(bf16[16,196,512]{2,1,0:T(8,128)(2,1)S(1)} %slice.33) | data formatting | bytes 6422528
  227.1 0.0 copy-done.1
  227.1 0.3 slice.34
  227.4 2.8 %copy.22 = bf16[16,196,512]{2,0,1:T(8,128)(2,1)} copy(bf16[16,196,512]{2,1,0:T(8,128)(2,1)S(1)} %slice.34) | data formatting | bytes 6422528
  (9 shorter events, 0.1 us)
Async XLA Ops:
  2.5 7.5 %copy-start = (bf16[16,196,512]{2,0,1:T(8,128)(2,1)S(1)}, bf16[16,196,512]{2,0,1:T(8,128)(2,1)}, u32[]{:S(2)}) copy-start(bf16[16,196,512]{2,0,1:T(8,128)(2,1)} %param.6) | copy-start | bytes 9633796
  224.3 2.8 %copy-start.1 = (bf16[16,208,512]{2,1,0:T(8,128)(2,1)S(1)}, bf16[16,208,512]{2,1,0:T(8,128)(2,1)}, u32[]{:S(2)}) copy-start(bf16[16,208,512]{2,1,0:T(8,128)(2,1)} %get-tuple-element.17) | copy-start | bytes 10223620

commit v2 on v1

--- a/solution.py
+++ b/solution.py
@@ -55,10 +55,10 @@
 
 
 def finish_rows(raw, back, pair):
+    total = pair + back
     inverse = inverse_norm(raw)
-    unit = raw * inverse
-    total = pair + back
-    return ((total - unit * jnp.sum(unit * total, axis=-1, keepdims=True)) * inverse).astype(BF16)
+    along = jnp.sum(raw * total, axis=-1, keepdims=True)
+    return ((total - raw * (inverse * inverse * along)) * inverse).astype(BF16)
 
 
 def kernel(
@@ -78,8 +78,13 @@
         x = (my_x + turn % SIDE) % SIDE
         return {"opt": z * SIDE + x}
 
-    def sar_peer(step):
-        return {"sar": (my_sar + step) % n_sar}
+    n_y = n_sar // 2
+    my_y, my_core = my_sar // 2, my_sar % 2
+
+    def y_peer(step):
+        return {"sar": ((my_y + step) % n_y) * 2 + my_core}
+
+    mate = {"sar": my_y * 2 + 1 - my_core}
 
     def remote(src, dst, send, recv, to):
         return pltpu.make_async_remote_copy(
@@ -92,10 +97,11 @@
         pl.semaphore_signal(
             barrier, inc=1, device_id=peer(turn), device_id_type=pl.DeviceIdType.MESH
         )
-    for step in range(1, n_sar):
+    for step in range(1, n_y):
         pl.semaphore_signal(
-            barrier, inc=1, device_id=sar_peer(step), device_id_type=pl.DeviceIdType.MESH
+            barrier, inc=1, device_id=y_peer(step), device_id_type=pl.DeviceIdType.MESH
         )
+    pl.semaphore_signal(barrier, inc=1, device_id=mate, device_id_type=pl.DeviceIdType.MESH)
 
     tail_buf[...] = jnp.zeros_like(tail_buf)
 
@@ -114,11 +120,11 @@
             means[which, pl.ds(i, 1), :] = mean
             return carry
 
-        lax.fori_loop(0, T, tile, 0)
+        lax.fori_loop(0, T, tile, 0, unroll=2)
 
     normalize(1, opt_raw, opt_rows)
 
-    pl.semaphore_wait(barrier, GROUPS - 1 + n_sar - 1)
+    pl.semaphore_wait(barrier, GROUPS - 1 + n_y)
 
     def ids_copy(turn):
         return remote(
@@ -146,7 +152,7 @@
                 dst = fetched_end.at[box, pl.ds(c * CHUNK - FIRST, CHUNK)]
         return remote(src, dst, fetch_send.at[turn, c], fetch_recv.at[turn, c], peer(turn))
 
-    for c in range(CHUNKS + 1):
+    def send_chunk(c):
         for turn in ORDER:
             asker = negated(turn)
             if c < CHUNKS:
@@ -161,6 +167,8 @@
                 out_tail[turn - 1] = jnp.concatenate(ends, axis=0).astype(BF16)
             fetch_copy(turn, c).start()
 
+    send_chunk(0)
+
     def clear(i, carry):
         sar_rows[i, ROWS:LANES] = jnp.zeros((LANES - ROWS, D), BF16)
         return carry
@@ -174,14 +182,16 @@
         pool_scale = lax.rsqrt(jnp.sum(mean * mean, axis=-1, keepdims=True) + EPSILON)
         pool = mean * pool_scale
         pool_rows[which] = pool
-        pools[my_sar, which, mine, :] = pool.astype(BF16)
+        pools[my_y, my_core, which, mine, :] = pool.astype(BF16)
 
     def plane_copy(turn):
-        here = pools.at[my_sar, :, mine, :]
+        here = pools.at[my_y, my_core, :, mine, :]
         return remote(here, here, plane_send.at[turn], plane_recv.at[turn], peer(turn))
 
     for turn in ORDER:
         plane_copy(turn).start()
+
+    send_chunk(1)
 
     def exp_scores(rows, i):
         return jnp.exp2(dot(rows, sar_rows[i], NT) * (LOG2E / POOL_TEMP))
@@ -233,19 +243,29 @@
         plane_copy(turn).wait_recv()
 
     def block_copy(step):
-        here = pools.at[my_sar]
-        return remote(here, here, block_send.at[step], block_recv.at[step], sar_peer(step))
-
-    for step in range(1, n_sar):
+        here = pools.at[my_y, my_core]
+        return remote(here, here, block_send.at[step], block_recv.at[step], y_peer(step))
+
+    def mate_copy(y):
+        here = pools.at[y, my_core]
+        return remote(here, here, block_send.at[n_y + y], block_recv.at[n_y + y], mate)
+
+    for step in range(1, n_y):
         block_copy(step).start()
+        if step + 1 < CHUNKS:
+            send_chunk(step + 1)
+    for c in range(n_y, CHUNKS + 1):
+        send_chunk(c)
 
     for c in range(FIRST // CHUNK):
         for turn in ORDER:
             fetch_copy(turn, c).wait_recv()
 
     def first_scores(i, carry):
+        rows = [fetched[table[SLOT_AT + i * NEG + k]] for k in range(NEG)]
+        exps = exp_scores(jnp.concatenate(rows, axis=0), i)
         for k in range(NEG):
-            e = exp_scores(fetched[table[SLOT_AT + i * NEG + k]], i)
+            e = exps[k * FIRST : (k + 1) * FIRST]
             weight[T + i * NEG + k, 0:FIRST] = e.astype(BF16)
             totals[k + 1, pl.ds(i, 1), :] = jnp.sum(e, axis=0, keepdims=True)
         return carry
@@ -266,15 +286,22 @@
     live_end = lax.broadcasted_iota(jnp.int32, (ROWS - FIRST, LANES), 0) < L - FIRST
 
     def last_scores(i, carry):
+        rows = [fetched_end[table[SLOT_AT + i * NEG + k]] for k in range(NEG)]
+        exps = exp_scores(jnp.concatenate(rows, axis=0), i)
         for k in range(NEG):
-            e = exp_scores(fetched_end[table[SLOT_AT + i * NEG + k]], i)
+            e = exps[k * (ROWS - FIRST) : (k + 1) * (ROWS - FIRST)]
             weight[T + i * NEG + k, FIRST:ROWS] = e.astype(BF16)
             totals[k + 1, pl.ds(i, 1), :] += jnp.sum(
                 jnp.where(live_end, e, 0.0), axis=0, keepdims=True
             )
         return carry
 
-    lax.fori_loop(0, T, last_scores, 0)
+    lax.fori_loop(0, T, last_scores, 0, unroll=2)
+
+    for step in range(1, n_y):
+        block_copy(step).wait_recv()
+    for y in range(n_y):
+        mate_copy(y).start()
 
     tokens = lax.broadcasted_iota(jnp.int32, (T, LANES), 1) < L
     cand = []
@@ -320,8 +347,20 @@
             parts[p] = total.astype(BF16)
             return carry
 
-        lax.fori_loop(0, PAIRS, add_pair, 0)
-
+        lax.fori_loop(0, PAIRS, add_pair, 0, unroll=2)
+
+        def send_tails(h=h, cols=cols):
+            for turn in ORDER:
+                ends = [
+                    parts[table[LAST_AT + (negated(turn) - 1) * CAP + s], MAIN:ROWS].astype(F32)[0:8]
+                    for s in range(CAP)
+                ]
+                out_tail[turn - 1, :, cols] = jnp.concatenate(ends, axis=0).astype(BF16)
+                if h:
+                    back_copy(turn, h, None).start()
+
+        if h:
+            send_tails()
         for c in range(CHUNKS):
             at = slice(c * CHUNK, (c + 1) * CHUNK)
             for turn in ORDER:
@@ -329,43 +368,37 @@
                     last = table[LAST_AT + (negated(turn) - 1) * CAP + s]
                     outbox[(turn - 1) * CAP + s, at, cols] = parts[last, at, :]
                 back_copy(turn, h, c).start()
-        for turn in ORDER:
-            ends = [
-                parts[table[LAST_AT + (negated(turn) - 1) * CAP + s], MAIN:ROWS].astype(F32)[0:8]
-                for s in range(CAP)
-            ]
-            out_tail[turn - 1, :, cols] = jnp.concatenate(ends, axis=0).astype(BF16)
-            if h:
-                back_copy(turn, h, None).start()
-
-    for step in range(1, n_sar):
-        block_copy(step).wait_recv()
-    block = pools.shape[2]
+        if not h:
+            send_tails()
+
+    for y in range(n_y):
+        mate_copy(y).wait_recv()
+    block = pools.shape[3]
     logit_scale = LOG2E / NCE_TEMP
-    own_sar = pools[my_sar, 0, mine, :]
-    own_opt = pools[my_sar, 1, mine, :]
+    own_sar = pools[my_y, my_core, 0, mine, :]
+    own_opt = pools[my_y, my_core, 1, mine, :]
 
     def own_rows(t, row_sums):
-        e = jnp.exp2(dot(own_sar, pools[t, 1], NT) * logit_scale)
+        e = jnp.exp2(dot(own_sar, pools[t // 2, t % 2, 1], NT) * logit_scale)
         return row_sums + jnp.sum(e, axis=-1, keepdims=True)
 
     row_sums = lax.fori_loop(0, n_sar, own_rows, jnp.zeros((T, 1), F32))
 
     def own_coefs(t, grad):
-        e = jnp.exp2(dot(own_sar, pools[t, 1], NT) * logit_scale)
+        e = jnp.exp2(dot(own_sar, pools[t // 2, t % 2, 1], NT) * logit_scale)
         rows = my_sar * block + me * T + lax.broadcasted_iota(jnp.int32, (T, block), 0)
         columns = t * block + lax.broadcasted_iota(jnp.int32, (T, block), 1)
         diagonal = (rows == columns).astype(F32)
         coefs = (NCE_SCALE * (e / row_sums - diagonal)).astype(BF16)
-        return grad + dot(coefs, pools[t, 1], NN)
+        return grad + dot(coefs, pools[t // 2, t % 2, 1], NN)
 
     sar_pool_grad = lax.fori_loop(0, n_sar, own_coefs, jnp.zeros((T, D), F32))
 
     def opt_coefs(s, grad):
-        rows_here = pools[s, 0]
+        rows_here = pools[s // 2, s % 2, 0]
 
         def add_sums(t, sums_here):
-            e = jnp.exp2(dot(rows_here, pools[t, 1], NT) * logit_scale)
+            e = jnp.exp2(dot(rows_here, pools[t // 2, t % 2, 1], NT) * logit_scale)
             return sums_here + jnp.sum(e, axis=-1, keepdims=True)
 
         sums_here = lax.fori_loop(0, n_sar, add_sums, jnp.zeros((block, 1), F32))
@@ -411,39 +444,6 @@
     sums[SLOTS] = jnp.zeros((CHUNK, D), F32)
     tail_sums[SLOTS] = jnp.zeros((8, D), F32)
     writes = []
-    for c in range(CHUNKS):
-        at = slice(c * CHUNK, (c + 1) * CHUNK)
-        for turn in ORDER:
-            back_copy(turn, 0, c).wait_recv()
-            back_copy(turn, 1, c).wait_recv()
-
-        def add_slot(t, total, c=c):
-            total = total * same2[t].astype(F32) + returned[c][order2[t]].astype(F32)
-            sums[t] = total
-            return total
-
-        lax.fori_loop(0, SLOTS, add_slot, jnp.zeros((CHUNK, D), F32))
-
-        if c * CHUNK < FIRST:
-            stage, stage_at = fetched, c * CHUNK
-        else:
-            stage, stage_at = fetched_end, c * CHUNK - FIRST
-
-        def opt_tile(j, carry, at=at, stage=stage, stage_at=stage_at):
-            pair = own_pair[j, at] + sums[last2[j]]
-            stage[j, stage_at : stage_at + CHUNK] = finish_rows(
-                opt_raw[j, at].astype(F32), backs[1, pl.ds(j, 1), :], pair
-            )
-            return carry
-
-        lax.fori_loop(0, T, opt_tile, 0)
-        rows_at = pl.ds(c * CHUNK, CHUNK)
-        write = pltpu.make_async_copy(
-            stage.at[pl.ds(0, T), pl.ds(stage_at, CHUNK)], opt_out.at[:, rows_at], write_sem.at[c]
-        )
-        write.start()
-        writes.append(write)
-
     for turn in ORDER:
         back_copy(turn, 1, None).wait_recv()
 
@@ -473,14 +473,49 @@
     write.start()
     writes.append(write)
 
+    for c in range(CHUNKS):
+        at = slice(c * CHUNK, (c + 1) * CHUNK)
+        for turn in ORDER:
+            back_copy(turn, 0, c).wait_recv()
+            back_copy(turn, 1, c).wait_recv()
+
+        def add_slot(t, total, c=c):
+            total = total * same2[t].astype(F32) + returned[c][order2[t]].astype(F32)
+            sums[t] = total
+            return total
+
+        lax.fori_loop(0, SLOTS, add_slot, jnp.zeros((CHUNK, D), F32), unroll=2)
+
+        if c * CHUNK < FIRST:
+            stage, stage_at = fetched, c * CHUNK
+        else:
+            stage, stage_at = fetched_end, c * CHUNK - FIRST
+
+        def opt_tile(j, carry, at=at, stage=stage, stage_at=stage_at):
+            pair = own_pair[j, at] + sums[last2[j]]
+            stage[j, stage_at : stage_at + CHUNK] = finish_rows(
+                opt_raw[j, at].astype(F32), backs[1, pl.ds(j, 1), :], pair
+            )
+            return carry
+
+        lax.fori_loop(0, T, opt_tile, 0, unroll=2)
+        rows_at = pl.ds(c * CHUNK, CHUNK)
+        write = pltpu.make_async_copy(
+            stage.at[pl.ds(0, T), pl.ds(stage_at, CHUNK)], opt_out.at[:, rows_at], write_sem.at[c]
+        )
+        write.start()
+        writes.append(write)
+
     for turn in ORDER:
         plane_copy(turn).wait_send()
         for c in range(CHUNKS):
             back_copy(turn, 0, c).wait_send()
             back_copy(turn, 1, c).wait_send()
         back_copy(turn, 1, None).wait_send()
-    for step in range(1, n_sar):
+    for step in range(1, n_y):
         block_copy(step).wait_send()
+    for y in range(n_y):
+        mate_copy(y).wait_send()
     write_sar.wait()
     for write in writes:
         write.wait()
@@ -546,7 +581,7 @@
             [pltpu.VMEM((SLOTS, CHUNK, D), BF16)] * CHUNKS,
             pltpu.VMEM((GROUPS - 1, 16, D), BF16),
             pltpu.VMEM((SLOTS + 1, 8, D), F32),
-            pltpu.VMEM((n_sar, 2, T * GROUPS, D), BF16),
+            pltpu.VMEM((n_sar // 2, 2, 2, T * GROUPS, D), BF16),
             pltpu.VMEM((SLOTS + 1, CHUNK, D), F32),
             pltpu.VMEM((T, ROWS, D), F32),
             pltpu.VMEM((2, T, D), F32),

time: 235 us -> 208 us (0.89); the launches traced: 230 us -> 208 us
  Pallas kernels: 209 us -> 186 us
    pallas_call x1, Pallas kernels: 209 us -> 186 us  [per_device(): pl.pallas_call(functools.partial(kernel, n_sar), out_shape=(padded, padde...]
where the time goes in v2:
time: 208 us
  Pallas kernels  186 us (89%)
  local copies, waits for them, and re-layouts  18.1 us (9%)
  other arithmetic  2.7 us (1%)
    pallas_call x1, Pallas kernels, per_device(): pl.pallas_call(functools.partial(kernel, n_sar), out_shape=(padded, padde...  186 us
    unnamed x8, local copies, waits for them, and re-layouts  14.6 us

profile of v2, /device:TPU:2, one launch (start us, length us, event | category | flops | bytes accessed | tf_op | source)
XLA Modules:
  0.0 208.0 jit_solution(14424288490843184371)
XLA Ops:
  0.7 0.7 add_select_fusion
  1.4 0.1 copy.17
  1.4 0.1 reshape.325
  1.5 0.1 convert_reduce_fusion
  1.6 0.1 fusion.1
  1.7 0.1 reshape.326
  1.8 0.2 reduce_window_sum.13
  2.0 0.1 reduce_window_sum.14
  2.0 0.2 select_reduce_fusion
  2.3 0.1 multiply_reduce_fusion.1
  2.4 0.1 multiply_reduce_fusion
  2.5 0.0 copy-start
  2.5 0.2 convert_reduce_fusion.1
  2.7 0.1 select_reduce_fusion.1
  2.8 0.1 fusion
  2.9 0.1 convert_reduce_fusion.2
  3.1 0.1 fusion.9
  3.2 0.1 concatenate.9
  3.3 0.6 convert_element_type.49.table
  3.9 0.1 copy.18
  3.9 0.6 scatter.4.ids
  4.5 5.4 %copy.19.sar_raw = bf16[16,196,512]{2,1,0:T(8,128)(2,1)} copy(bf16[16,196,512]{2,0,1:T(8,128)(2,1)} %param.5) | data formatting | bytes 6422528 | tf_op args[0]
  10.0 0.0 copy-done
  10.0 3.6 %copy.20.opt_raw = bf16[16,196,512]{2,1,0:T(8,128)(2,1)} copy(bf16[16,196,512]{2,0,1:T(8,128)(2,1)S(1)} %copy-done) | data formatting | bytes 6422528 | tf_op args[1]
  13.5 186.4 %match_grads.1 = (bf16[16,208,512]{2,1,0:T(8,128)(2,1)}, bf16[16,208,512]{2,1,0:T(8,128)(2,1)}) custom-call(s32[256]{0:T(256)} %convert_element_type.49.table, s32[16,1,128]{2,1,0:T(1,128)} %scatter.4.ids, bf16[16,196,512]{2,1,0:T(8,128)(2,1)} %copy.19.sar_raw, bf16[16,196,512]{2,1,0:T(8,128)(2,1)} %copy.20.opt_raw), custom_call_target="tpu_custom_call" | custom-call | tf_op jit(solution)/shard_map/match_grads/pallas_call | solution.py:565
  200.0 2.1 %slice.33 = bf16[16,196,512]{2,1,0:T(8,128)(2,1)S(1)} slice(bf16[16,208,512]{2,1,0:T(8,128)(2,1)} %get-tuple-element.16), slice={[0:16], [0:196], [0:512]} | slice | bytes 6422528 | tf_op jit(solution)/shard_map/slice | solution.py:618
  202.1 0.0 copy-start.1
  202.1 2.8 %copy.21 = bf16[16,196,512]{2,0,1:T(8,128)(2,1)} copy(bf16[16,196,512]{2,1,0:T(8,128)(2,1)S(1)} %slice.33) | data formatting | bytes 6422528
  204.9 0.0 copy-done.1
  204.9 0.3 slice.34
  205.2 2.8 %copy.22 = bf16[16,196,512]{2,0,1:T(8,128)(2,1)} copy(bf16[16,196,512]{2,1,0:T(8,128)(2,1)S(1)} %slice.34) | data formatting | bytes 6422528
  (9 shorter events, 0.1 us)
Async XLA Ops:
  2.5 7.5 %copy-start = (bf16[16,196,512]{2,0,1:T(8,128)(2,1)S(1)}, bf16[16,196,512]{2,0,1:T(8,128)(2,1)}, u32[]{:S(2)}) copy-start(bf16[16,196,512]{2,0,1:T(8,128)(2,1)} %param.6) | copy-start | bytes 9633796
  202.1 2.8 %copy-start.1 = (bf16[16,208,512]{2,1,0:T(8,128)(2,1)S(1)}, bf16[16,208,512]{2,1,0:T(8,128)(2,1)}, u32[]{:S(2)}) copy-start(bf16[16,208,512]{2,1,0:T(8,128)(2,1)} %get-tuple-element.17) | copy-start | bytes 10223620

commit v3 on v2

--- a/solution.py
+++ b/solution.py
@@ -62,12 +62,12 @@
 
 
 def kernel(
-    n_sar, table, ids, sar_raw, opt_raw, sar_out, opt_out,
-    sar_rows, opt_rows, outbox, out_tail, fetched, fetched_end, fetched_tail, weight, parts, acc,
-    returned, returned_tail, tail_sums, pools, sums, own_pair, means, pool_rows, backs, totals,
-    scale, tail_buf, ids_in, ids_smem, keys, ranks, order2, same2, last2,
+    n_sar, table, ids, sar_in, opt_in, sar_out, opt_out,
+    sar_raw, opt_raw, sar_rows, opt_rows, outbox, out_tail, fetched, fetched_end, fetched_tail, weight, parts, acc,
+    returned, returned_tail, low_ends, tail_sums, pools, sums, own_pair, means, pool_rows, backs, totals,
+    scale, ids_in, ids_smem, keys, ranks, order2, same2, last2,
     ids_send, ids_recv, ids_sem, fetch_send, fetch_recv, back_send, back_recv,
-    plane_send, plane_recv, block_send, block_recv, write_sem,
+    plane_send, plane_recv, block_send, block_recv, write_sem, read_sem,
 ):
     my_sar = lax.axis_index("sar")
     me = lax.axis_index("opt")
@@ -103,26 +103,63 @@
         )
     pl.semaphore_signal(barrier, inc=1, device_id=mate, device_id_type=pl.DeviceIdType.MESH)
 
-    tail_buf[...] = jnp.zeros_like(tail_buf)
-
-    def normalize(which, raw, rows):
+    def reads(which, source, rows):
+        span = rows.shape[1]
+        copies = []
+        for k in range(-(-T * L // span)):
+            size = min(span, T * L - k * span)
+            copies.append(
+                pltpu.make_async_copy(
+                    source.at[pl.ds(k * span, size)],
+                    rows.at[k, pl.ds(0, size)],
+                    read_sem.at[which, k],
+                )
+            )
+        return copies
+
+    opt_reads, sar_reads = reads(1, opt_in, opt_rows), reads(0, sar_in, sar_rows)
+    for copy in opt_reads + sar_reads:
+        copy.start()
+
+    def put_rows(at, values):
+        for q in range(D // 128):
+            own_pair[q, at] = values[:, q * 128 : (q + 1) * 128]
+
+    def get_rows(at):
+        return jnp.concatenate([own_pair[q, at] for q in range(D // 128)], axis=1)
+
+    put_rows(pl.ds(T * L, T * (ROWS - L)), jnp.zeros((T * (ROWS - L), D), F32))
+
+    def widen_all(copies, rows):
+        span = rows.shape[1]
+        for copy in copies:
+            copy.wait()
+
+        def widen(k, carry):
+            put_rows(pl.ds(pl.multiple_of(k * span, 16), span), rows[k].astype(F32))
+            return carry
+
+        full = T * L // span
+        rest = T * L - full * span
+        lax.fori_loop(0, full, widen, 0)
+        put_rows(pl.ds(full * span, rest), rows[full, 0:rest].astype(F32))
+
+    def normalize(which, raw, rows, first, size):
         def tile(i, carry):
-            main = raw[i, 0:MAIN].astype(F32)
-            tail_buf[0:4] = raw[i, MAIN:L].astype(F32)
-            tail = tail_buf[...]
-            unit = main * inverse_norm(main)
-            unit_tail = tail * inverse_norm(tail)
-            rows[i, 0:MAIN] = unit.astype(BF16)
-            rows[i, MAIN:ROWS] = unit_tail.astype(BF16)
-            mean = (
-                jnp.sum(unit, axis=0, keepdims=True) + jnp.sum(unit_tail, axis=0, keepdims=True)
-            ) * (1.0 / L)
-            means[which, pl.ds(i, 1), :] = mean
+            values = get_rows(pl.ds(first * T + i, size, stride=T))
+            unit = values * inverse_norm(values)
+            raw[i, first : first + size] = values.astype(BF16)
+            rows[i, first : first + size] = unit.astype(BF16)
+            mean = jnp.sum(unit, axis=0, keepdims=True) * (1.0 / L)
+            if first == 0:
+                means[which, pl.ds(i, 1), :] = mean
+            else:
+                means[which, pl.ds(i, 1), :] += mean
             return carry
 
         lax.fori_loop(0, T, tile, 0, unroll=2)
 
-    normalize(1, opt_raw, opt_rows)
+    widen_all(opt_reads, opt_rows)
 
     pl.semaphore_wait(barrier, GROUPS - 1 + n_y)
 
@@ -133,6 +170,7 @@
 
     for turn in ORDER:
         ids_copy(turn).start()
+    normalize(1, opt_raw, opt_rows, 0, CHUNK)
     for turn in ORDER:
         ids_copy(turn).wait()
     to_smem = pltpu.make_async_copy(ids_in, ids_smem, ids_sem)
@@ -152,6 +190,17 @@
                 dst = fetched_end.at[box, pl.ds(c * CHUNK - FIRST, CHUNK)]
         return remote(src, dst, fetch_send.at[turn, c], fetch_recv.at[turn, c], peer(turn))
 
+    def pack_ends(low, high):
+        upper = lax.broadcasted_iota(jnp.int32, (16, HALF), 0) % 8 < 4
+        return jnp.where(upper, low, pltpu.roll(high, 4, 0)).astype(BF16)
+
+    def unpack_ends(packed):
+        upper = lax.broadcasted_iota(jnp.int32, (16, HALF), 0) % 8 < 4
+        packed = packed.astype(F32)
+        low = jnp.where(upper, packed, 0.0)
+        high = jnp.where(upper, pltpu.roll(packed, 12, 0), 0.0)
+        return jnp.concatenate([low, high], axis=1)
+
     def send_chunk(c):
         for turn in ORDER:
             asker = negated(turn)
@@ -164,17 +213,21 @@
                 ends = [
                     opt_rows[ids_smem[asker, 0, s], MAIN:ROWS].astype(F32)[0:8] for s in range(CAP)
                 ]
-                out_tail[turn - 1] = jnp.concatenate(ends, axis=0).astype(BF16)
+                both = jnp.concatenate(ends, axis=0)
+                out_tail[turn - 1] = pack_ends(both[:, :HALF], both[:, HALF:])
             fetch_copy(turn, c).start()
 
     send_chunk(0)
+
+    normalize(1, opt_raw, opt_rows, CHUNK, ROWS - CHUNK)
+    widen_all(sar_reads, sar_rows)
+    normalize(0, sar_raw, sar_rows, 0, ROWS)
 
     def clear(i, carry):
         sar_rows[i, ROWS:LANES] = jnp.zeros((LANES - ROWS, D), BF16)
         return carry
 
     lax.fori_loop(0, T, clear, 0)
-    normalize(0, sar_raw, sar_rows)
 
     mine = pl.ds(pl.multiple_of(me * T, T), T)
     for which in range(2):
@@ -276,7 +329,7 @@
         for turn in ORDER:
             fetch_copy(turn, c).wait_recv()
     for turn in range(1, GROUPS):
-        ends = fetched_tail[turn - 1].astype(F32)
+        ends = unpack_ends(fetched_tail[turn - 1])
         for s in range(CAP):
             end = ends[8 * s : 8 * s + 8]
             fetched_end[(turn - 1) * CAP + s, MAIN - FIRST :] = jnp.concatenate(
@@ -355,9 +408,12 @@
                     parts[table[LAST_AT + (negated(turn) - 1) * CAP + s], MAIN:ROWS].astype(F32)[0:8]
                     for s in range(CAP)
                 ]
-                out_tail[turn - 1, :, cols] = jnp.concatenate(ends, axis=0).astype(BF16)
+                both = jnp.concatenate(ends, axis=0)
                 if h:
+                    out_tail[turn - 1] = pack_ends(low_ends[turn - 1], both)
                     back_copy(turn, h, None).start()
+                else:
+                    low_ends[turn - 1] = both
 
         if h:
             send_tails()
@@ -418,13 +474,12 @@
         along = jnp.sum(pool * grad, axis=-1, keepdims=True)
         backs[which] = (grad - pool * along) * pool_scale * (1.0 / L)
 
-    def raw_tail(raw, i):
-        tail_buf[0:4] = raw[i, MAIN:L].astype(F32)
-        return tail_buf[...]
+    def own_at(i, size=ROWS, first=0):
+        return pl.ds(pl.multiple_of(i * ROWS + first, 16), size)
 
     def sar_tile(i, carry):
         own = weights(i)
-        own_pair[i] = dot(own, sar_rows[i], NN)
+        put_rows(own_at(i), dot(own, sar_rows[i], NN))
         cands = [opt_rows[i]]
         coefs = [own]
         for k in range(NEG):
@@ -433,8 +488,7 @@
             coefs.append(weights(T + i * NEG + k))
         pair = dot(jnp.concatenate(coefs, axis=0), jnp.concatenate(cands, axis=0), TN)
         back = backs[0, pl.ds(i, 1), :]
-        opt_rows[i, 0:MAIN] = finish_rows(sar_raw[i, 0:MAIN].astype(F32), back, pair[0:MAIN])
-        opt_rows[i, MAIN:ROWS] = finish_rows(raw_tail(sar_raw, i), back, pair[MAIN:ROWS])
+        opt_rows[i] = finish_rows(sar_raw[i].astype(F32), back, pair[0:ROWS])
         return carry
 
     lax.fori_loop(0, T, sar_tile, 0)
@@ -449,7 +503,7 @@
 
     def add_tail(t, total):
         place = order2[t]
-        both = returned_tail[place // CAP].astype(F32)
+        both = unpack_ends(returned_tail[place // CAP])
         second = (place % CAP).astype(F32)
         total = total * same2[t].astype(F32) + both[0:8] * (1.0 - second) + both[8:16] * second
         tail_sums[t] = total
@@ -459,8 +513,10 @@
 
     def opt_tail(j, carry):
         part = tail_sums[last2[j]]
-        pair = own_pair[j, MAIN:ROWS] + jnp.concatenate([part, jnp.zeros_like(part)], axis=0)
-        fetched_end[j, MAIN - FIRST :] = finish_rows(raw_tail(opt_raw, j), backs[1, pl.ds(j, 1), :], pair)
+        pair = get_rows(own_at(j, ROWS - MAIN, MAIN)) + jnp.concatenate([part, jnp.zeros_like(part)], axis=0)
+        fetched_end[j, MAIN - FIRST :] = finish_rows(
+            opt_raw[j, MAIN:ROWS].astype(F32), backs[1, pl.ds(j, 1), :], pair
+        )
         return carry
 
     lax.fori_loop(0, T, opt_tail, 0)
@@ -491,8 +547,8 @@
         else:
             stage, stage_at = fetched_end, c * CHUNK - FIRST
 
-        def opt_tile(j, carry, at=at, stage=stage, stage_at=stage_at):
-            pair = own_pair[j, at] + sums[last2[j]]
+        def opt_tile(j, carry, c=c, at=at, stage=stage, stage_at=stage_at):
+            pair = get_rows(own_at(j, CHUNK, c * CHUNK)) + sums[last2[j]]
             stage[j, stage_at : stage_at + CHUNK] = finish_rows(
                 opt_raw[j, at].astype(F32), backs[1, pl.ds(j, 1), :], pair
             )
@@ -557,39 +613,46 @@
     return table.astype(jnp.int32), ids
 
 
+def by_token(tokens):
+    return jnp.swapaxes(tokens, 0, 1).reshape(-1, D)
+
+
 def per_device(n_sar, sar_tokens, opt_tokens, candidates):
     table, ids = index_tables(candidates)
     vmem = pl.BlockSpec(memory_space=pltpu.VMEM)
+    hbm = pl.BlockSpec(memory_space=pl.ANY)
     dma = pltpu.SemaphoreType.DMA
     padded = jax.ShapeDtypeStruct((T, ROWS, D), BF16)
     grads = pl.pallas_call(
         functools.partial(kernel, n_sar),
         out_shape=(padded, padded),
-        in_specs=[pl.BlockSpec(memory_space=pltpu.SMEM), vmem, vmem, vmem],
-        out_specs=[pl.BlockSpec(memory_space=pl.ANY)] * 2,
+        in_specs=[pl.BlockSpec(memory_space=pltpu.SMEM), vmem, hbm, hbm],
+        out_specs=[hbm] * 2,
         scratch_shapes=[
+            pltpu.VMEM((T, ROWS, D), BF16),
+            pltpu.VMEM((T, ROWS, D), BF16),
             pltpu.VMEM((T, LANES, D), BF16),
             pltpu.VMEM((T, ROWS, D), BF16),
             pltpu.VMEM((SLOTS, MAIN, D), BF16),
-            pltpu.VMEM((GROUPS - 1, 16, D), BF16),
+            pltpu.VMEM((GROUPS - 1, 16, HALF), BF16),
             pltpu.VMEM((SLOTS, FIRST, D), BF16),
             pltpu.VMEM((SLOTS, ROWS - FIRST, D), BF16),
-            pltpu.VMEM((GROUPS - 1, 16, D), BF16),
+            pltpu.VMEM((GROUPS - 1, 16, HALF), BF16),
             pltpu.VMEM((T + PAIRS, ROWS, LANES), BF16),
             pltpu.VMEM((PAIRS + 1, ROWS, HALF), BF16),
             pltpu.VMEM((ROWS, HALF), F32),
             [pltpu.VMEM((SLOTS, CHUNK, D), BF16)] * CHUNKS,
-            pltpu.VMEM((GROUPS - 1, 16, D), BF16),
+            pltpu.VMEM((GROUPS - 1, 16, HALF), BF16),
+            pltpu.VMEM((GROUPS - 1, 16, HALF), F32),
             pltpu.VMEM((SLOTS + 1, 8, D), F32),
             pltpu.VMEM((n_sar // 2, 2, 2, T * GROUPS, D), BF16),
             pltpu.VMEM((SLOTS + 1, CHUNK, D), F32),
-            pltpu.VMEM((T, ROWS, D), F32),
+            pltpu.VMEM((D // 128, T * ROWS, 128), F32),
             pltpu.VMEM((2, T, D), F32),
             pltpu.VMEM((2, T, D), F32),
             pltpu.VMEM((2, T, D), F32),
             pltpu.VMEM((NEG + 1, T, LANES), F32),
             pltpu.VMEM((T + PAIRS, 1, LANES), F32),
-            pltpu.VMEM((16, D), F32),
             pltpu.VMEM((GROUPS, 1, 128), jnp.int32),
             pltpu.SMEM((GROUPS, 1, 128), jnp.int32),
             pltpu.SMEM((32,), jnp.int32),
@@ -609,12 +672,13 @@
             dma((n_sar,)),
             dma((n_sar,)),
             dma((CHUNKS + 2,)),
+            dma((2, T)),
         ],
         compiler_params=pltpu.CompilerParams(
             collective_id=0, has_side_effects=True, vmem_limit_bytes=63 * 2**20
         ),
         name="match_grads",
-    )(table, ids, sar_tokens, opt_tokens)
+    )(table, ids, by_token(sar_tokens), by_token(opt_tokens))
     return tuple(grad[:, :L] for grad in grads)
 
 

time: 208 us -> 194 us (0.933)
  local copies, waits for them, and re-layouts: 18.1 us -> 9.1 us
  Pallas kernels: 186 us -> 181 us
    unnamed x8 -> x4, local copies, waits for them, and re-layouts: 14.6 us -> 5.6 us
    pallas_call x1, Pallas kernels: 186 us -> 181 us  [per_device(): pl.pallas_call(functools.partial(kernel, n_sar), out_shape=(padded, padde...]
where the time goes in v3:
time: 194 us
  Pallas kernels  181 us (93%)
  local copies, waits for them, and re-layouts  9.1 us (5%)
  other arithmetic  2.71 us (1%)
    pallas_call x1, Pallas kernels, per_device(): pl.pallas_call(functools.partial(kernel, n_sar), out_shape=(padded, padde...  181 us
    unnamed x4, local copies, waits for them, and re-layouts  5.6 us

profile of v3, /device:TPU:2, one launch (start us, length us, event | category | flops | bytes accessed | tf_op | source)
XLA Modules:
  0.0 193.8 jit_solution(10794339171844211364)
XLA Ops:
  0.7 0.7 add_select_fusion
  1.4 0.1 copy.13
  1.4 0.1 reshape.331
  1.5 0.1 convert_reduce_fusion
  1.6 0.1 fusion.1
  1.7 0.1 reshape.332
  1.8 0.2 reduce_window_sum.13
  2.0 0.1 reduce_window_sum.14
  2.0 0.2 select_reduce_fusion
  2.3 0.1 multiply_reduce_fusion.1
  2.4 0.1 multiply_reduce_fusion
  2.5 0.2 convert_reduce_fusion.1
  2.7 0.1 select_reduce_fusion.1
  2.8 0.1 fusion
  2.9 0.1 convert_reduce_fusion.2
  3.1 0.1 fusion.9
  3.2 0.1 concatenate.9
  3.3 0.6 convert_element_type.49.table
  3.9 0.1 copy.14
  3.9 0.6 scatter.4.ids
  4.5 181.3 %match_grads.1 = (bf16[16,208,512]{2,1,0:T(8,128)(2,1)}, bf16[16,208,512]{2,1,0:T(8,128)(2,1)}) custom-call(s32[256]{0:T(256)} %convert_element_type.49.table, s32[16,1,128]{2,1,0:T(1,128)} %scatter.4.ids, bf16[3136,512]{1,0:T(8,128)(2,1)} %bitcast.8, bf16[3136,512]{1,0:T(8,128)(2,1)} %bitcast.9), custom_call_target="tpu_custom_call" | custom-call | tf_op jit(solution)/shard_map/match_grads/pallas_call | solution.py:626
  185.8 2.1 %slice.33 = bf16[16,196,512]{2,1,0:T(8,128)(2,1)S(1)} slice(bf16[16,208,512]{2,1,0:T(8,128)(2,1)} %get-tuple-element.16), slice={[0:16], [0:196], [0:512]} | slice | bytes 6422528 | tf_op jit(solution)/shard_map/slice | solution.py:682
  188.0 0.0 copy-start
  188.0 2.8 %copy.15 = bf16[16,196,512]{2,0,1:T(8,128)(2,1)} copy(bf16[16,196,512]{2,1,0:T(8,128)(2,1)S(1)} %slice.33) | data formatting | bytes 6422528
  190.8 0.0 copy-done
  190.8 0.3 slice.34
  191.0 2.8 %copy.16 = bf16[16,196,512]{2,0,1:T(8,128)(2,1)} copy(bf16[16,196,512]{2,1,0:T(8,128)(2,1)S(1)} %slice.34) | data formatting | bytes 6422528
  (9 shorter events, 0.1 us)
Async XLA Ops:
  188.0 2.8 %copy-start = (bf16[16,208,512]{2,1,0:T(8,128)(2,1)S(1)}, bf16[16,208,512]{2,1,0:T(8,128)(2,1)}, u32[]{:S(2)}) copy-start(bf16[16,208,512]{2,1,0:T(8,128)(2,1)} %get-tuple-element.17) | copy-start | bytes 10223620

commit v4 on v3

--- a/solution.py
+++ b/solution.py
@@ -58,14 +58,14 @@
     total = pair + back
     inverse = inverse_norm(raw)
     along = jnp.sum(raw * total, axis=-1, keepdims=True)
-    return ((total - raw * (inverse * inverse * along)) * inverse).astype(BF16)
+    return (total - raw * (inverse * inverse * along)) * inverse
 
 
 def kernel(
     n_sar, table, ids, sar_in, opt_in, sar_out, opt_out,
     sar_raw, opt_raw, sar_rows, opt_rows, outbox, out_tail, fetched, fetched_end, fetched_tail, weight, parts, acc,
     returned, returned_tail, low_ends, tail_sums, pools, sums, own_pair, means, pool_rows, backs, totals,
-    scale, ids_in, ids_smem, keys, ranks, order2, same2, last2,
+    scale, by_row, staged, ids_in, ids_smem, keys, ranks, order2, same2, last2,
     ids_send, ids_recv, ids_sem, fetch_send, fetch_recv, back_send, back_recv,
     plane_send, plane_recv, block_send, block_recv, write_sem, read_sem,
 ):
@@ -488,16 +488,45 @@
             coefs.append(weights(T + i * NEG + k))
         pair = dot(jnp.concatenate(coefs, axis=0), jnp.concatenate(cands, axis=0), TN)
         back = backs[0, pl.ds(i, 1), :]
-        opt_rows[i] = finish_rows(sar_raw[i].astype(F32), back, pair[0:ROWS])
+        opt_rows[i] = finish_rows(sar_raw[i].astype(F32), back, pair[0:ROWS]).astype(BF16)
         return carry
 
     lax.fori_loop(0, T, sar_tile, 0)
-    write_sar = pltpu.make_async_copy(opt_rows, sar_out, write_sem.at[CHUNKS + 1])
-    write_sar.start()
+
+    def put_grad(i, values):
+        size = values.shape[0]
+        for q in range(D // 128):
+            by_row[q, pl.ds(i, size, stride=T)] = values[:, q * 128 : (q + 1) * 128]
+
+    writes = []
+
+    def write_grad(which, out, c):
+        size = T * (CHUNK if c < CHUNKS else L - MAIN)
+        if len(writes) > 1:
+            writes[-2].wait()
+        slot = len(writes) % 2
+        for q in range(D // 128):
+            staged[slot, 0:size, q * 128 : (q + 1) * 128] = by_row[q, 0:size].astype(BF16)
+        write = pltpu.make_async_copy(
+            staged.at[slot, pl.ds(0, size)],
+            out.at[pl.ds(c * CHUNK * T, size)],
+            write_sem.at[which, c],
+        )
+        write.start()
+        writes.append(write)
+
+    for c in range(CHUNKS + 1):
+        at = slice(c * CHUNK, min((c + 1) * CHUNK, ROWS))
+
+        def place_tile(i, carry, at=at):
+            put_grad(i, opt_rows[i, at].astype(F32))
+            return carry
+
+        lax.fori_loop(0, T, place_tile, 0, unroll=2)
+        write_grad(0, sar_out, c)
 
     sums[SLOTS] = jnp.zeros((CHUNK, D), F32)
     tail_sums[SLOTS] = jnp.zeros((8, D), F32)
-    writes = []
     for turn in ORDER:
         back_copy(turn, 1, None).wait_recv()
 
@@ -514,20 +543,12 @@
     def opt_tail(j, carry):
         part = tail_sums[last2[j]]
         pair = get_rows(own_at(j, ROWS - MAIN, MAIN)) + jnp.concatenate([part, jnp.zeros_like(part)], axis=0)
-        fetched_end[j, MAIN - FIRST :] = finish_rows(
-            opt_raw[j, MAIN:ROWS].astype(F32), backs[1, pl.ds(j, 1), :], pair
-        )
+        back = backs[1, pl.ds(j, 1), :]
+        put_grad(j, finish_rows(opt_raw[j, MAIN:ROWS].astype(F32), back, pair))
         return carry
 
     lax.fori_loop(0, T, opt_tail, 0)
-    rows_at = pl.ds(MAIN, ROWS - MAIN)
-    write = pltpu.make_async_copy(
-        fetched_end.at[pl.ds(0, T), pl.ds(MAIN - FIRST, ROWS - MAIN)],
-        opt_out.at[:, rows_at],
-        write_sem.at[CHUNKS],
-    )
-    write.start()
-    writes.append(write)
+    write_grad(1, opt_out, CHUNKS)
 
     for c in range(CHUNKS):
         at = slice(c * CHUNK, (c + 1) * CHUNK)
@@ -542,25 +563,14 @@
 
         lax.fori_loop(0, SLOTS, add_slot, jnp.zeros((CHUNK, D), F32), unroll=2)
 
-        if c * CHUNK < FIRST:
-            stage, stage_at = fetched, c * CHUNK
-        else:
-            stage, stage_at = fetched_end, c * CHUNK - FIRST
-
-        def opt_tile(j, carry, c=c, at=at, stage=stage, stage_at=stage_at):
+        def opt_tile(j, carry, c=c, at=at):
             pair = get_rows(own_at(j, CHUNK, c * CHUNK)) + sums[last2[j]]
-            stage[j, stage_at : stage_at + CHUNK] = finish_rows(
-                opt_raw[j, at].astype(F32), backs[1, pl.ds(j, 1), :], pair
-            )
+            back = backs[1, pl.ds(j, 1), :]
+            put_grad(j, finish_rows(opt_raw[j, at].astype(F32), back, pair))
             return carry
 
         lax.fori_loop(0, T, opt_tile, 0, unroll=2)
-        rows_at = pl.ds(c * CHUNK, CHUNK)
-        write = pltpu.make_async_copy(
-            stage.at[pl.ds(0, T), pl.ds(stage_at, CHUNK)], opt_out.at[:, rows_at], write_sem.at[c]
-        )
-        write.start()
-        writes.append(write)
+        write_grad(1, opt_out, c)
 
     for turn in ORDER:
         plane_copy(turn).wait_send()
@@ -572,8 +582,7 @@
         block_copy(step).wait_send()
     for y in range(n_y):
         mate_copy(y).wait_send()
-    write_sar.wait()
-    for write in writes:
+    for write in writes[-2:]:
         write.wait()
 
 
@@ -584,7 +593,7 @@
     hits = (local_ids[:, None] == jnp.arange(block)[None, :]).astype(jnp.int32)
     needed = jnp.max(hits, axis=0).reshape(GROUPS, T)
     rank = jnp.cumsum(needed, axis=1) - needed
-    chosen = needed[:, :, None] * (rank[:, :, None] == jnp.arange(CAP)[None, None, :])
+    chosen = needed[:, :, None] * (rank[:, :, None] == jnp.arange(128)[None, None, :])
     asked = jnp.sum(chosen * jnp.arange(T)[None, :, None], axis=1)
     pair_rank = jnp.sum(hits * rank.reshape(-1)[None, :], axis=1)
     owner = local_ids // T
@@ -595,7 +604,7 @@
     by_turn = jnp.sum(
         (owners[:, None] == jnp.arange(GROUPS)[None, :])[:, :, None] * asked[None], axis=1
     )
-    ids = jnp.zeros((GROUPS, 1, 128), jnp.int32).at[:, 0, :CAP].set(by_turn)
+    ids = by_turn.astype(jnp.int32)[:, None, :]
     pairs = jnp.arange(PAIRS)
     key = slot * 64 + pairs
     place = jnp.sum(key[None, :] < key[:, None], axis=1)
@@ -608,7 +617,7 @@
     used = jnp.any(slot[None, :] == slots[:, None], axis=1)
     last = jnp.where(used, upto - 1, PAIRS)
     table = jnp.concatenate(
-        [slot, sorted_pair, sorted_pair // NEG, same, last, jnp.zeros((TABLE - LAST_AT - SLOTS,))]
+        [slot, sorted_pair, sorted_pair // NEG, same, last, jnp.zeros((TABLE - LAST_AT - SLOTS,), jnp.int32)]
     )
     return table.astype(jnp.int32), ids
 
@@ -622,10 +631,10 @@
     vmem = pl.BlockSpec(memory_space=pltpu.VMEM)
     hbm = pl.BlockSpec(memory_space=pl.ANY)
     dma = pltpu.SemaphoreType.DMA
-    padded = jax.ShapeDtypeStruct((T, ROWS, D), BF16)
+    rows = jax.ShapeDtypeStruct((T * L, D), BF16)
     grads = pl.pallas_call(
         functools.partial(kernel, n_sar),
-        out_shape=(padded, padded),
+        out_shape=(rows, rows),
         in_specs=[pl.BlockSpec(memory_space=pltpu.SMEM), vmem, hbm, hbm],
         out_specs=[hbm] * 2,
         scratch_shapes=[
@@ -653,6 +662,8 @@
             pltpu.VMEM((2, T, D), F32),
             pltpu.VMEM((NEG + 1, T, LANES), F32),
             pltpu.VMEM((T + PAIRS, 1, LANES), F32),
+            pltpu.VMEM((D // 128, T * CHUNK, 128), F32),
+            pltpu.VMEM((2, T * CHUNK, D), BF16),
             pltpu.VMEM((GROUPS, 1, 128), jnp.int32),
             pltpu.SMEM((GROUPS, 1, 128), jnp.int32),
             pltpu.SMEM((32,), jnp.int32),
@@ -671,7 +682,7 @@
             dma((GROUPS,)),
             dma((n_sar,)),
             dma((n_sar,)),
-            dma((CHUNKS + 2,)),
+            dma((2, CHUNKS + 1)),
             dma((2, T)),
         ],
         compiler_params=pltpu.CompilerParams(
@@ -679,7 +690,7 @@
         ),
         name="match_grads",
     )(table, ids, by_token(sar_tokens), by_token(opt_tokens))
-    return tuple(grad[:, :L] for grad in grads)
+    return tuple(jnp.swapaxes(grad.reshape(L, T, D), 0, 1) for grad in grads)
 
 
 def solution(mesh):

time: 194 us -> 193 us (level)
  local copies, waits for them, and re-layouts: 9.1 us -> 6.74 us
    slice x2 -> x0, local copies, waits for them, and re-layouts: 2.4 us -> none  [per_device(): return tuple((grad[:, :L] for grad in grads))]
where the time goes in v4:
time: 193 us; the launch traced here: 192 us
  Pallas kernels  182 us (94%)
  local copies, waits for them, and re-layouts  6.74 us (3%)
  other arithmetic  2.75 us (1%)
    pallas_call x1, Pallas kernels, per_device(): pl.pallas_call(functools.partial(kernel, n_sar), out_shape=(rows, rows),...  182 us
    unnamed x4, local copies, waits for them, and re-layouts  5.76 us

profile of v4, /device:TPU:2, one launch (start us, length us, event | category | flops | bytes accessed | tf_op | source)
XLA Modules:
  0.0 192.2 jit_solution(1776372273779562005)
XLA Ops:
  0.7 0.7 add_select_fusion
  1.4 0.1 copy.7
  1.4 0.1 reshape.299
  1.5 0.1 convert_reduce_fusion
  1.6 0.1 fusion.1
  1.7 0.1 reshape.300
  1.8 0.2 reduce_window_sum.13
  2.0 0.1 reduce_window_sum.14
  2.0 0.2 select_reduce_fusion
  2.3 0.1 multiply_reduce_fusion.1
  2.4 0.7 multiply_reduce_fusion
  3.1 0.2 convert_reduce_fusion.1
  3.3 0.1 select_reduce_fusion.1
  3.4 0.1 fusion
  3.6 0.1 convert_reduce_fusion.2
  3.7 0.1 compare_convert_fusion
  3.8 0.6 concatenate.7.table
  4.4 182.0 %match_grads.1 = (bf16[3136,512]{1,0:T(8,128)(2,1)}, bf16[3136,512]{1,0:T(8,128)(2,1)}) custom-call(s32[256]{0:T(256)} %concatenate.7.table, s32[16,1,128]{2,1,0:T(1,128)} %bitcast.18, bf16[3136,512]{1,0:T(8,128)(2,1)} %bitcast.14, bf16[3136,512]{1,0:T(8,128)(2,1)} %bitcast.15), custom_call_target="tpu_custom_call" | custom-call | tf_op jit(solution)/shard_map/match_grads/pallas_call | solution.py:635
  186.4 0.0 copy-start
  186.4 4.1 %copy.10 = bf16[16,196,512]{2,0,1:T(8,128)(2,1)} copy(bf16[16,196,512]{2,0,1:T(8,128)(2,1)} %bitcast.17) | data formatting | bytes 6422528
  190.5 0.0 copy-done
  190.5 1.7 copy.11
  (7 shorter events, 0.1 us)
Async XLA Ops:
  186.4 4.1 %copy-start = (bf16[3136,512]{1,0:T(8,128)(2,1)S(1)}, bf16[3136,512]{1,0:T(8,128)(2,1)}, u32[]{:S(2)}) copy-start(bf16[3136,512]{1,0:T(8,128)(2,1)} %get-tuple-element.5) | copy-start | bytes 9633796

commit v5 on v4

--- a/solution.py
+++ b/solution.py
@@ -349,7 +349,7 @@
             )
         return carry
 
-    lax.fori_loop(0, T, last_scores, 0, unroll=2)
+    lax.fori_loop(0, T, last_scores, 0, unroll=4)
 
     for step in range(1, n_y):
         block_copy(step).wait_recv()
@@ -400,7 +400,7 @@
             parts[p] = total.astype(BF16)
             return carry
 
-        lax.fori_loop(0, PAIRS, add_pair, 0, unroll=2)
+        lax.fori_loop(0, PAIRS, add_pair, 0, unroll=4)
 
         def send_tails(h=h, cols=cols):
             for turn in ORDER:
@@ -569,7 +569,7 @@
             put_grad(j, finish_rows(opt_raw[j, at].astype(F32), back, pair))
             return carry
 
-        lax.fori_loop(0, T, opt_tile, 0, unroll=2)
+        lax.fori_loop(0, T, opt_tile, 0, unroll=4)
         write_grad(1, opt_out, c)
 
     for turn in ORDER:

time: 193 us -> 190 us (0.984)
  Pallas kernels: 182 us -> 179 us
    pallas_call x1, Pallas kernels: 182 us -> 179 us  [per_device(): pl.pallas_call(functools.partial(kernel, n_sar), out_shape=(rows, rows),...]
where the time goes in v5:
time: 190 us; the launch traced here: 189 us
  Pallas kernels  179 us (94%)
  local copies, waits for them, and re-layouts  6.74 us (4%)
  other arithmetic  2.75 us (1%)
    pallas_call x1, Pallas kernels, per_device(): pl.pallas_call(functools.partial(kernel, n_sar), out_shape=(rows, rows),...  179 us
    unnamed x4, local copies, waits for them, and re-layouts  5.76 us

profile of v5, /device:TPU:2, one launch (start us, length us, event | category | flops | bytes accessed | tf_op | source)
XLA Modules:
  0.0 189.1 jit_solution(15947944816380556954)
XLA Ops:
  0.7 0.7 add_select_fusion
  1.4 0.1 copy.7
  1.4 0.1 reshape.299
  1.5 0.1 convert_reduce_fusion
  1.6 0.1 fusion.1
  1.7 0.1 reshape.300
  1.8 0.2 reduce_window_sum.13
  2.0 0.1 reduce_window_sum.14
  2.0 0.2 select_reduce_fusion
  2.3 0.1 multiply_reduce_fusion.1
  2.4 0.7 multiply_reduce_fusion
  3.1 0.2 convert_reduce_fusion.1
  3.3 0.1 select_reduce_fusion.1
  3.4 0.1 fusion
  3.6 0.1 convert_reduce_fusion.2
  3.7 0.1 compare_convert_fusion
  3.8 0.6 concatenate.7.table
  4.4 178.9 %match_grads.1 = (bf16[3136,512]{1,0:T(8,128)(2,1)}, bf16[3136,512]{1,0:T(8,128)(2,1)}) custom-call(s32[256]{0:T(256)} %concatenate.7.table, s32[16,1,128]{2,1,0:T(1,128)} %bitcast.18, bf16[3136,512]{1,0:T(8,128)(2,1)} %bitcast.14, bf16[3136,512]{1,0:T(8,128)(2,1)} %bitcast.15), custom_call_target="tpu_custom_call" | custom-call | tf_op jit(solution)/shard_map/match_grads/pallas_call | solution.py:635
  183.4 0.0 copy-start
  183.4 4.1 %copy.10 = bf16[16,196,512]{2,0,1:T(8,128)(2,1)} copy(bf16[16,196,512]{2,0,1:T(8,128)(2,1)} %bitcast.17) | data formatting | bytes 6422528
  187.4 0.0 copy-done
  187.4 1.7 copy.11
  (7 shorter events, 0.1 us)
Async XLA Ops:
  183.4 4.1 %copy-start = (bf16[3136,512]{1,0:T(8,128)(2,1)S(1)}, bf16[3136,512]{1,0:T(8,128)(2,1)}, u32[]{:S(2)}) copy-start(bf16[3136,512]{1,0:T(8,128)(2,1)} %get-tuple-element.5) | copy-start | bytes 9633796
